TPU v7x, 256 devices: a whole 4x4x8 slice. The times are simulated.
256 devices in a mesh: grp: 16 (over y_hi, z), dev: 16 (over y_lo, x, core).
Axes of the slice: x: 4, y: 4 (y_hi: 2, y_lo: 2; y = y_hi * 2 + y_lo), z: 8, core: 2. Of those that a mesh axis runs over, the one named last changes fastest.
Arguments:
- spatial_basis: bfloat16 [2, 32, 2, 192, 192], P(None, None, None, 'dev'), may hold values from -6 to 6
- temporal: bfloat16 [2, 32, 256], replicated, may hold values from -1 to 1
- coil_maps: bfloat16 [2, 16, 2, 192, 192], replicated, may hold values from -1.5 to 1.5
- kspace_data: float32 [256, 2, 16, 2, 48, 192], P(('grp', 'dev')), may hold values from -6 to 6
- sampled_lines: int32 [256, 48], P(('grp', 'dev')), may hold values from 0 to 191, as said below
Outputs:
- updated_basis: float32 [2, 32, 2, 192, 192], P(None, None, None, 'dev', 'grp')
Inputs may be any that keep to these rules, and one draw needn't show every extreme that they name: `sampled_lines`: each row holds 48 different line indices of one frame.
All inputs are finite; a program needn't handle non-finite values.
Results may differ from a plain program's by a relative error of at most 0.0004.
Values may be sent and summed in bfloat16 or wider, within the bound.
No kernel may reach another device: no remote copies, remote signals or barrier semaphores. Data moves between devices by JAX's collectives and lax.ppermute only.
A program may use at most 128 MiB of HBM per device.

v0:
```python
import math

import jax
import jax.numpy as jnp
import numpy as np
from jax import lax
from jax.experimental import pallas as pl
from jax.experimental.pallas import tpu as pltpu
from jax.sharding import PartitionSpec as P

STEP_SIZE = 0.25
N = 192
PART = 12
RANK = 32
COILS = 16
LINES = 48
GROUP = 16
VOX = 2 * 2 * PART * PART
WIDE = 640
F32 = jnp.float32
BF16 = jnp.bfloat16
VMEM = pl.BlockSpec(memory_space=pltpu.VMEM)


def two_terms(values):
    high = values.astype(np.float32).astype(jnp.bfloat16)
    low = (values - high.astype(np.float64)).astype(jnp.bfloat16)
    return high, low


def split(values):
    high = values.astype(BF16)
    return high, (values - high.astype(F32)).astype(BF16)


def dot(left, right, over=(1, 0)):
    return lax.dot_general(
        left, right, (((over[0],), (over[1],)), ((), ())), preferred_element_type=F32
    )


def constants():
    places = np.arange(N)
    angles = (places[:, None] * places[None, :] % N) * (2.0 * math.pi / N)
    cos_pair = two_terms(np.cos(angles) / math.sqrt(N))
    sin_pair = two_terms(np.sin(angles) / math.sqrt(N))
    dft = np.stack([*cos_pair, *sin_pair])
    columns = np.arange(2 * RANK * 2 * PART)
    spread = (columns[None, :] // (2 * PART) == np.arange(2 * RANK)[:, None])
    rows = np.arange(2 * PART)
    inside = (columns[None, :] % (2 * PART) == ((rows % PART) * 2 + rows // PART)[:, None])
    order = np.arange(N)
    depth_order = ((order % GROUP) * PART + order // GROUP)[:, None] == places[None, :]
    wide = np.arange(4 * N)
    target = (wide // PART % GROUP) * (4 * PART) + (wide // N) * PART + wide % PART
    lane_order = target[:, None] == wide[None, :]
    peers = np.arange(GROUP * GROUP)
    frame_order = ((peers % GROUP) * GROUP + peers // GROUP)[:, None] == peers[None, :]
    out = np.arange(2 * PART * PART)
    row, zz, pos = out // (2 * PART), out // 2 % PART, out % 2
    pick = np.stack(
        [
            (zz * 48 + part * 24 + pos * PART + row)[:, None] == np.arange(WIDE)[None, :]
            for part in range(2)
        ]
    )
    return dict(
        dft=dft,
        spread=spread.astype(jnp.bfloat16),
        inside=inside.astype(np.float32),
        depth_order=depth_order.astype(jnp.bfloat16),
        lane_order=lane_order.astype(jnp.bfloat16),
        frame_order=frame_order.astype(jnp.bfloat16),
        pick=pick.astype(jnp.bfloat16),
    )


def frames_kernel(basis_ref, temporal_ref, spread_ref, inside_ref, out_ref, mix_ref):
    first = lax.axis_index("grp") * GROUP
    frame = lax.broadcasted_iota(jnp.int32, (GROUP, GROUP * GROUP), 0) + first
    column = lax.broadcasted_iota(jnp.int32, (GROUP, GROUP * GROUP), 1)
    chosen = (frame == column).astype(F32).astype(BF16)
    weights = dot(chosen, temporal_ref[...], (1, 1))
    lane = lax.broadcasted_iota(jnp.int32, (GROUP, 2 * RANK), 1)
    from_lane = lax.broadcasted_iota(jnp.int32, (2 * RANK, 2 * RANK), 0)
    to_lane = lax.broadcasted_iota(jnp.int32, (2 * RANK, 2 * RANK), 1)
    apart = jnp.abs(from_lane - to_lane) == RANK
    swapped = dot(weights.astype(BF16), apart.astype(F32).astype(BF16))
    signed = jnp.where(lane < RANK, weights, -weights)
    wide_re = dot(signed.astype(BF16), spread_ref[...])
    wide_im = dot(swapped.astype(BF16), spread_ref[...])
    inside = inside_ref[...]
    for f in range(GROUP):
        block = jnp.concatenate(
            [inside * wide_re[f : f + 1], inside * wide_im[f : f + 1]], axis=0
        )
        mix_ref[f * 48 : (f + 1) * 48, :] = block.astype(BF16)
    images = dot(mix_ref[...], basis_ref[...])
    for f in range(GROUP):
        image = images[f * 48 : (f + 1) * 48]
        out_ref[f, 0:48, :] = image[:, 0:128]
        out_ref[f, 48:72, 0:64] = image[0:24, 128:192]
        out_ref[f, 48:72, 64:128] = image[24:48, 128:192]


def frames(basis, temporal, spread, inside):
    rows = 2 * RANK * 2 * PART
    return pl.pallas_call(
        frames_kernel,
        out_shape=jax.ShapeDtypeStruct((GROUP, 72, 128), F32),
        in_specs=[VMEM] * 4,
        out_specs=VMEM,
        scratch_shapes=[pltpu.VMEM((GROUP * 48, rows), BF16)],
        compiler_params=pltpu.CompilerParams(vmem_limit_bytes=24 * 1024 * 1024),
        name="frames",
    )(basis, temporal, spread, inside)


def data_kernel(
    data_ref, lines_ref, dft_ref, temporal_ref, order_ref,
    back_ref, ahead_ref, adjoint_ref, low_ref, weights_ref,
):
    step = pl.program_id(0)

    @pl.when(step == 0)
    def tables():
        places = lax.broadcasted_iota(jnp.int32, (N, LINES), 0)
        chosen = (places == lines_ref[...]).astype(F32)
        chosen_rows = chosen.T.astype(BF16)
        chosen = chosen.astype(BF16)
        for term in range(2):
            cos_line = dot(chosen_rows, dft_ref[term])
            sin_line = dot(chosen_rows, dft_ref[2 + term])
            at = term * 96
            ahead_ref[at : at + 96, 0:N] = jnp.concatenate([cos_line, -sin_line], 0).astype(BF16)
            ahead_ref[at : at + 96, N : 2 * N] = jnp.concatenate([sin_line, cos_line], 0).astype(BF16)
            cos_back = dot(dft_ref[term], chosen)
            sin_back = dot(dft_ref[2 + term], chosen)
            full = jnp.concatenate(
                [
                    jnp.concatenate([cos_back, -sin_back], 1),
                    jnp.concatenate([sin_back, cos_back], 1),
                ],
                0,
            ).astype(BF16)
            if term == 0:
                adjoint_ref[:, 0:96] = full
                adjoint_ref[:, 96:192] = full
            else:
                low_ref[...] = full
        weights_ref[...] = dot(order_ref[...], temporal_ref[...], (1, 1)).astype(BF16)

    coils_here = data_ref.shape[2]
    data_re = data_ref[0, 0].reshape(coils_here * 2 * LINES, N)
    data_im = data_ref[0, 1].reshape(coils_here * 2 * LINES, N)
    re_high, re_low = split(data_re)
    im_high, im_low = split(data_im)

    def through(high, low, which):
        return (
            dot(high, dft_ref[which])
            + dot(low, dft_ref[which])
            + dot(high, dft_ref[which + 1])
        )

    back_re = through(re_high, re_low, 0) - through(im_high, im_low, 2)
    back_im = through(re_high, re_low, 2) + through(im_high, im_low, 0)
    back_ref[:, 0:LINES, :] = back_re.reshape(coils_here * 2, LINES, N)
    back_ref[:, LINES : 2 * LINES, :] = back_im.reshape(coils_here * 2, LINES, N)


def data_back(data, lines, dft, temporal, order):
    coils_here = 4
    whole = lambda *shape: pl.BlockSpec(shape, lambda i: (0,) * len(shape))
    return pl.pallas_call(
        data_kernel,
        grid=(COILS // coils_here,),
        out_shape=(
            jax.ShapeDtypeStruct((COILS * 2, 2 * LINES, N), F32),
            jax.ShapeDtypeStruct((4 * LINES, 2 * N), BF16),
            jax.ShapeDtypeStruct((2 * N, 4 * LINES), BF16),
            jax.ShapeDtypeStruct((2 * N, 2 * LINES), BF16),
            jax.ShapeDtypeStruct((GROUP * GROUP, 2 * RANK), BF16),
        ),
        in_specs=[
            pl.BlockSpec((1, 2, coils_here, 2, LINES, N), lambda i: (0, 0, i, 0, 0, 0)),
            whole(1, LINES),
            whole(4, N, N),
            whole(2 * RANK, GROUP * GROUP),
            whole(GROUP * GROUP, GROUP * GROUP),
        ],
        out_specs=(
            pl.BlockSpec((coils_here * 2, 2 * LINES, N), lambda i: (i, 0, 0)),
            whole(4 * LINES, 2 * N),
            whole(2 * N, 4 * LINES),
            whole(2 * N, 2 * LINES),
            whole(GROUP * GROUP, 2 * RANK),
        ),
        compiler_params=pltpu.CompilerParams(vmem_limit_bytes=24 * 1024 * 1024),
        name="data_back",
    )(data, lines, dft, temporal, order)


def model_kernel(
    images_ref, coils_ref, back_ref, ahead_ref, adjoint_ref, low_ref,
    depth_ref, lane_ref, out_ref, field_ref, grad_ref,
):
    for d in range(GROUP):
        at = d * PART
        for part in range(2):
            for pos in range(2):
                row = part * 24 + pos * PART
                field_ref[part, pos, at : at + PART, 0:128] = images_ref[d, row : row + PART, :]
                tail = 48 + pos * PART
                field_ref[part, pos, at : at + PART, 128:N] = images_ref[
                    d, tail : tail + PART, part * 64 : part * 64 + 64
                ]
    grad_ref[...] = jnp.zeros_like(grad_ref)
    for pos in range(2):

        def one_coil(coil, carry):
            coil_re = coils_ref[0, coil, pos].astype(F32)
            coil_im = coils_ref[1, coil, pos].astype(F32)
            field_re = field_ref[0, pos]
            field_im = field_ref[1, pos]
            re_high, re_low = split(coil_re * field_re - coil_im * field_im)
            im_high, im_low = split(coil_re * field_im + coil_im * field_re)
            high = jnp.concatenate([re_high, im_high], 0)
            low = jnp.concatenate([re_low, im_low], 0)
            first = dot(ahead_ref[...], high)
            lines = first[0:96] + first[96:192] + dot(ahead_ref[0:96, :], low)
            resid_high, resid_low = split(lines - back_ref[coil * 2 + pos])
            rows = dot(adjoint_ref[...], jnp.concatenate([resid_high, resid_low], 0))
            rows = rows + dot(low_ref[...], resid_high)
            rows_re, rows_im = rows[0:N], rows[N : 2 * N]
            grad_ref[0, pos] += coil_re * rows_re + coil_im * rows_im
            grad_ref[1, pos] += coil_re * rows_im - coil_im * rows_re
            return carry

        lax.fori_loop(0, COILS, one_coil, 0)
    highs, lows = [], []
    for part in range(2):
        for pos in range(2):
            high, low = split(grad_ref[part, pos])
            highs.append(dot(depth_ref[...], high, (1, 1)).astype(BF16))
            lows.append(dot(depth_ref[...], low, (1, 1)).astype(BF16))
    total = jnp.zeros((N, 4 * N), F32)
    for channel in range(4):
        order = lane_ref[channel * N : (channel + 1) * N, :]
        total = total + dot(highs[channel], order) + dot(lows[channel], order)
    for d in range(GROUP):
        out_ref[d * GROUP : (d + 1) * GROUP, 0:VOX] = jnp.concatenate(
            [total[zz * GROUP : (zz + 1) * GROUP, d * 48 : (d + 1) * 48] for zz in range(PART)], 1
        )
    out_ref[:, VOX:WIDE] = jnp.zeros((GROUP * GROUP, WIDE - VOX), F32)


def model(images, coils, back, ahead, adjoint, low, depth_order, lane_order):
    return pl.pallas_call(
        model_kernel,
        out_shape=jax.ShapeDtypeStruct((GROUP * GROUP, WIDE), F32),
        in_specs=[VMEM] * 8,
        out_specs=VMEM,
        scratch_shapes=[
            pltpu.VMEM((2, 2, N, N), F32),
            pltpu.VMEM((2, 2, N, N), F32),
        ],
        compiler_params=pltpu.CompilerParams(vmem_limit_bytes=40 * 1024 * 1024),
        name="model",
    )(images, coils, back, ahead, adjoint, low, depth_order, lane_order)


def update_kernel(grads_ref, weights_ref, pick_ref, slab_ref, out_ref):
    high, low = split(grads_ref[...].T)
    weights = weights_ref[...]
    both = dot(high, weights) + dot(low, weights)
    high, low = split(both)
    from_re = dot(pick_ref[0], high) + dot(pick_ref[0], low)
    from_im = dot(pick_ref[1], high) + dot(pick_ref[1], low)
    grad_re = from_re[:, 0:RANK] + from_im[:, RANK : 2 * RANK]
    grad_im = from_im[:, 0:RANK] - from_re[:, RANK : 2 * RANK]
    out_ref[0] = slab_ref[0] - STEP_SIZE * grad_re
    out_ref[1] = slab_ref[1] - STEP_SIZE * grad_im


def update(grads, weights, pick, slab):
    return pl.pallas_call(
        update_kernel,
        out_shape=jax.ShapeDtypeStruct((2, 2 * PART * PART, RANK), F32),
        in_specs=[VMEM] * 4,
        out_specs=VMEM,
        compiler_params=pltpu.CompilerParams(vmem_limit_bytes=16 * 1024 * 1024),
        name="update",
    )(grads, weights, pick, slab)


def on_device(spatial_basis, temporal, coil_maps, kspace_data, sampled_lines):
    table = {name: jnp.asarray(value) for name, value in constants().items()}
    flat_temporal = temporal.reshape(2 * RANK, GROUP * GROUP)
    flat_basis = jnp.transpose(spatial_basis, (0, 1, 3, 2, 4)).reshape(-1, N)
    sent = frames(flat_basis, flat_temporal, table["spread"], table["inside"])
    images = lax.all_to_all(sent, "dev", 0, 0, tiled=True)
    back, ahead, adjoint, low, weights = data_back(
        kspace_data, sampled_lines, table["dft"], flat_temporal, table["frame_order"]
    )
    sent = model(
        images, coil_maps, back, ahead, adjoint, low, table["depth_order"], table["lane_order"]
    )
    grads = lax.all_to_all(
        sent.reshape(GROUP * GROUP, 1, WIDE), ("dev", "grp"), 0, 0, tiled=True
    )
    slab = lax.dynamic_slice_in_dim(spatial_basis, lax.axis_index("grp") * PART, PART, 4)
    slab = jnp.transpose(slab, (0, 3, 4, 2, 1)).reshape(2, 2 * PART * PART, RANK).astype(F32)
    result = update(grads.reshape(GROUP * GROUP, WIDE), weights, table["pick"], slab)
    return jnp.transpose(result.reshape(2, PART, PART, 2, RANK), (0, 4, 3, 1, 2))


def solution(mesh):
    placed = (
        P(None, None, None, "dev", None),
        P(),
        P(),
        P(("grp", "dev"), None, None, None, None, None),
        P(("grp", "dev"), None),
    )
    return jax.shard_map(
        on_device,
        mesh=mesh,
        in_specs=placed,
        out_specs=P(None, None, None, "dev", "grp"),
        check_vma=False,
    )
```

profile of v0, /device:TPU:1, one launch (start us, length us, event | category | flops | bytes accessed | tf_op | source)
XLA Modules:
  0.0 96.7 jit_solution(13224599252297668926)
XLA Ops:
  0.0 0.0 copy-start.4
  0.0 0.0 copy-start.19
  0.0 2.3 %reshape.18.basis_ref = bf16[1536,192]{1,0:T(8,128)(2,1)S(1)} reshape(bf16[2,32,12,2,192]{4,3,2,1,0:T(2,128)(2,1)} %bitcast.17) | data formatting | bytes 1179648 | tf_op jit(solution)/shard_map/reshape | solution.py:300
  2.3 0.0 copy-start.5
  2.3 0.9 copy-done.5
  3.3 0.0 copy-start.8
  3.3 0.9 copy-done.8
  4.2 0.0 copy-start.11
  4.2 0.8 copy-done.11
  4.9 2.0 %frames.1 = f32[16,72,128]{2,1,0:T(8,128)} custom-call(bf16[1536,192]{1,0:T(8,128)(2,1)S(1)} %reshape.18.basis_ref, bf16[64,256]{1,0:T(8,128)(2,1)S(1)} %bitcast.15, bf16[64,1536]{1,0:T(8,128)(2,1)S(1)} %copy-done.5, f32[24,1536]{1,0:T(8,128)S(1)} %copy-done.8), custom_call_target="tpu_custom_call" | custom-call | tf_op jit(solution)/shard_map/frames/pallas_call | solution.py:108
  7.0 7.2 %all-to-all-start = ((f32[16,72,128]{2,1,0:T(8,128)}), f32[16,72,128]{2,1,0:T(8,128)}, u32[]{:S(2)}, u32[]{:S(2)}) async-start(f32[16,72,128]{2,1,0:T(8,128)} %frames.1), calls=%async_computation | async-start | bytes 1179648 | tf_op jit(solution)/shard_map/all_to_all | solution.py:302
  14.2 0.0 copy-done.4
  14.2 0.0 copy-done.19
  14.2 0.0 copy-start.1
  14.2 1.9 %copy-done.1 = f32[1,2,16,2,48,192]{5,4,3,2,1,0:T(8,128)S(1)} copy-done((f32[1,2,16,2,48,192]{5,4,3,2,1,0:T(8,128)S(1)}, f32[1,2,16,2,48,192]{5,4,3,2,1,0:T(8,128)}, u32[]{:S(2)}) %copy-start.1) | copy-done | bytes 2359320
  16.1 0.0 copy-start.12
  16.1 0.8 copy-done.12
  16.9 0.0 copy-start.13
  16.9 0.9 copy-done.13
  17.8 3.9 %data_back.1 = (f32[32,96,192]{2,1,0:T(8,128)S(1)}, bf16[192,384]{1,0:T(8,128)(2,1)S(1)}, bf16[384,192]{1,0:T(8,128)(2,1)S(1)}, bf16[384,96]{1,0:T(8,128)(2,1)S(1)}, bf16[256,64]{1,0:T(8,128)(2,1)S(1)}) custom-call(f32[1,2,16,2,48,192]{5,4,3,2,1,0:T(8,128)S(1)} %copy-done.1, s32[1,48]{1,0:T(1,128)S(1)} %copy-done.19, bf16[4,192,192]{2,1,0:T(8,128)(2,1)S(1)} %copy-done.4, ...), custom_call_target="tpu_custom_call" | custom-call | tf_op jit(solution)/shard_map/data_back/pallas_call | solution.py:175
  21.6 0.0 copy-start.6
  21.7 0.7 copy-done.6
  22.3 0.0 copy-start.9
  22.3 0.7 copy-done.9
  23.0 0.0 copy-start.15
  23.0 0.6 copy-done.15
  23.6 0.0 copy-start.17
  23.6 0.6 copy-done.17
  24.2 0.8 all-to-all-done.images_ref
  25.1 0.0 copy-start
  25.1 2.8 %copy-done = bf16[2,16,2,192,192]{4,3,2,1,0:T(8,128)(2,1)S(1)} copy-done((bf16[2,16,2,192,192]{4,3,2,1,0:T(8,128)(2,1)S(1)}, bf16[2,16,2,192,192]{4,3,2,1,0:T(8,128)(2,1)}, u32[]{:S(2)}) %copy-start) | copy-done | bytes 4718616
  27.9 0.0 copy-start.2
  27.9 1.3 %copy-done.2 = bf16[768,768]{1,0:T(8,128)(2,1)S(1)} copy-done((bf16[768,768]{1,0:T(8,128)(2,1)S(1)}, bf16[768,768]{1,0:T(8,128)(2,1)}, u32[]{:S(2)}) %copy-start.2) | copy-done | bytes 1179672
  29.1 0.9 copy-done.7
  30.1 0.9 copy-done.10
  31.0 0.9 copy-done.14
  31.9 0.9 copy-done.16
  32.8 23.6 %model.1 = f32[256,640]{1,0:T(8,128)S(1)} custom-call(f32[16,72,128]{2,1,0:T(8,128)} %all-to-all-done.images_ref, bf16[2,16,2,192,192]{4,3,2,1,0:T(8,128)(2,1)S(1)} %copy-done, f32[32,96,192]{2,1,0:T(8,128)S(1)} %get-tuple-element.10.back_ref, bf16[192,384]{1,0:T(8,128)(2,1)S(1)} %copy-done.10, bf16[384,192]{1,0:T(8,128)(2,1)S(1)} %copy-done.7, ...), custom_call_target="tpu_custom_call" | custom-call | tf_op jit(solution)/shard_map/model/pallas_call | solution.py:259
  56.4 0.0 copy-start.3
  56.4 0.0 copy-start.18
  56.4 1.5 %copy.15 = f32[256,1,640]{2,1,0:T(1,128)} copy(f32[256,1,640]{2,0,1:T(8,128)S(1)} %bitcast.12) | data formatting | bytes 1310720 | tf_op jit(solution)/shard_map/reshape | solution.py:310
  58.0 13.1 %all-to-all-start.1 = ((f32[256,1,640]{2,1,0:T(1,128)}), f32[256,1,640]{2,1,0:T(1,128)S(1)}, u32[]{:S(2)}, u32[]{:S(2)}) async-start(f32[256,1,640]{2,1,0:T(1,128)} %copy.15), calls=%async_computation.1 | async-start | bytes 1310720 | tf_op jit(solution)/shard_map/all_to_all | solution.py:309
  71.1 1.6 %convert_bitcast_fusion = f32[2,12,12,2,32]{2,3,1,4,0:T(2,128)S(1)} fusion(bf16[2,32,2,12,192]{4,2,3,1,0:T(2,128)(2,1)} %param.12, s32[]{:T(128)S(6)} %select_n.3), kind=kLoop, calls=%fused_computation | loop fusion | flops 18432 | bytes 110596 | tf_op jit(solution)/shard_map/convert_element_type | solution.py:313
  72.8 0.5 copy.16
  73.3 21.5 %all-to-all-done.1 = f32[256,1,640]{2,1,0:T(1,128)S(1)} async-done(((f32[256,1,640]{2,1,0:T(1,128)}), f32[256,1,640]{2,1,0:T(1,128)S(1)}, u32[]{:S(2)}, u32[]{:S(2)}) %all-to-all-start.1) | async-done | bytes 655392 | tf_op jit(solution)/shard_map/all_to_all | solution.py:309
  94.8 0.0 copy-done.3
  94.8 0.0 copy-done.18
  94.9 1.9 %update.1 = f32[2,288,32]{2,1,0:T(8,128)} custom-call(f32[256,640]{1,0:T(8,128)S(1)} %bitcast.13, bf16[256,64]{1,0:T(8,128)(2,1)S(1)} %copy-done.18, bf16[2,288,640]{2,1,0:T(8,128)(2,1)S(1)} %copy-done.3, f32[2,288,32]{2,1,0:T(8,128)S(1)} %bitcast.14), custom_call_target="tpu_custom_call" | custom-call | tf_op jit(solution)/shard_map/update/pallas_call | solution.py:287
  (5 shorter events, 0.0 us)
Async XLA Ops:
  0.0 14.2 %copy-start.4 = (bf16[4,192,192]{2,1,0:T(8,128)(2,1)S(1)}, bf16[4,192,192]{2,1,0:T(8,128)(2,1)}, u32[]{:S(2)}) copy-start(bf16[4,192,192]{2,1,0:T(8,128)(2,1)} %constant.25.clone.dft_ref) | copy-start | bytes 884740
  0.0 14.2 %copy-start.19 = (s32[1,48]{1,0:T(1,128)S(1)}, s32[1,48]{1,0:T(1,128)}, u32[]{:S(2)}) copy-start(s32[1,48]{1,0:T(1,128)} %lines_ref.1) | copy-start | bytes 580
  2.3 0.9 copy-start.5
  3.3 0.9 copy-start.8
  4.2 0.8 copy-start.11
  7.0 18.1 %all-to-all-start = ((f32[16,72,128]{2,1,0:T(8,128)}), f32[16,72,128]{2,1,0:T(8,128)}, u32[]{:S(2)}, u32[]{:S(2)}) async-start(f32[16,72,128]{2,1,0:T(8,128)} %frames.1), calls=%async_computation | async-start | bytes 1179648 | tf_op jit(solution)/shard_map/all_to_all | solution.py:302
  14.2 1.9 %copy-start.1 = (f32[1,2,16,2,48,192]{5,4,3,2,1,0:T(8,128)S(1)}, f32[1,2,16,2,48,192]{5,4,3,2,1,0:T(8,128)}, u32[]{:S(2)}) copy-start(f32[1,2,16,2,48,192]{5,4,3,2,1,0:T(8,128)} %data_ref.1) | copy-start | bytes 7077892
  16.1 0.8 copy-start.12
  16.9 0.9 copy-start.13
  21.6 0.7 copy-start.6
  22.3 0.7 copy-start.9
  23.0 0.6 copy-start.15
  23.6 0.6 copy-start.17
  25.1 2.8 %copy-start = (bf16[2,16,2,192,192]{4,3,2,1,0:T(8,128)(2,1)S(1)}, bf16[2,16,2,192,192]{4,3,2,1,0:T(8,128)(2,1)}, u32[]{:S(2)}) copy-start(bf16[2,16,2,192,192]{4,3,2,1,0:T(8,128)(2,1)} %coils_ref.1) | copy-start | bytes 14155780
  27.9 1.3 %copy-start.2 = (bf16[768,768]{1,0:T(8,128)(2,1)S(1)}, bf16[768,768]{1,0:T(8,128)(2,1)}, u32[]{:S(2)}) copy-start(bf16[768,768]{1,0:T(8,128)(2,1)} %constant.29.clone.lane_ref) | copy-start | bytes 3538948
  29.1 0.9 copy-start.7
  30.1 0.9 copy-start.10
  31.0 0.9 copy-start.14
  31.9 0.9 copy-start.16
  56.4 38.4 %copy-start.3 = (bf16[2,288,640]{2,1,0:T(8,128)(2,1)S(1)}, bf16[2,288,640]{2,1,0:T(8,128)(2,1)}, u32[]{:S(2)}) copy-start(bf16[2,288,640]{2,1,0:T(8,128)(2,1)} %constant.31.clone.pick_ref) | copy-start | bytes 2211844
  56.4 38.4 %copy-start.18 = (bf16[256,64]{1,0:T(8,128)(2,1)S(1)}, bf16[256,64]{1,0:T(8,128)(2,1)}, u32[]{:S(2)}) copy-start(bf16[256,64]{1,0:T(8,128)(2,1)} %copy-done.17) | copy-start | bytes 98308
  58.0 36.8 %all-to-all-start.1 = ((f32[256,1,640]{2,1,0:T(1,128)}), f32[256,1,640]{2,1,0:T(1,128)S(1)}, u32[]{:S(2)}, u32[]{:S(2)}) async-start(f32[256,1,640]{2,1,0:T(1,128)} %copy.15), calls=%async_computation.1 | async-start | bytes 1310720 | tf_op jit(solution)/shard_map/all_to_all | solution.py:309
where the time goes:
time: 97.5 us; the launch traced here: 96.7 us
  Pallas kernels  31.4 us (32%)
  waiting for transfers between devices  22.3 us (23%)
  local copies, waits for them, and re-layouts  20.8 us (21%)
  starting transfers between devices  20.4 us (21%)
  other arithmetic  1.65 us (2%)
    pallas_call x1, Pallas kernels, model(): pl.pallas_call(model_kernel, out_shape=jax.ShapeDtypeStruct((GROUP * GROU...  23.6 us
    all_to_all x1, waiting for transfers between devices, on_device(): lax.all_to_all(sent.reshape(GROUP * GROUP, 1, WIDE), ('dev', 'grp'), 0, 0...  21.5 us
    unnamed x41, local copies, waits for them, and re-layouts  16.5 us
    all_to_all x1, starting transfers between devices, on_device(): lax.all_to_all(sent.reshape(GROUP * GROUP, 1, WIDE), ('dev', 'grp'), 0, 0...  13.1 us
    all_to_all x1, starting transfers between devices, on_device(): images = lax.all_to_all(sent, 'dev', 0, 0, tiled=True)  7.23 us
    pallas_call x1, Pallas kernels, data_back(): pl.pallas_call(data_kernel, grid=(COILS // coils_here,), out_shape=(jax.S...  3.86 us
    reshape x1, local copies, waits for them, and re-layouts, on_device(): flat_basis = jnp.transpose(spatial_basis, (0, 1, 3, 2, 4)).reshape(-1, N)  2.31 us
    pallas_call x1, Pallas kernels, frames(): pl.pallas_call(frames_kernel, out_shape=jax.ShapeDtypeStruct((GROUP, 72,...  2.05 us
  transfers between devices with their start and end apart: 2, of which 2 were waited for; matrix products, arithmetic and copies ran while one was open for 2% of the time, Pallas kernels for 4%

commit v1 on v0

--- a/solution.py
+++ b/solution.py
@@ -14,12 +14,18 @@
 RANK = 32
 COILS = 16
 LINES = 48
+CHUNK = 4
 GROUP = 16
 VOX = 2 * 2 * PART * PART
 WIDE = 640
 F32 = jnp.float32
 BF16 = jnp.bfloat16
 VMEM = pl.BlockSpec(memory_space=pltpu.VMEM)
+HBM = pl.BlockSpec(memory_space=pltpu.HBM)
+in_hbm = lambda array: pltpu.with_memory_space_constraint(array, pltpu.HBM)
+in_vmem = lambda array: pltpu.with_memory_space_constraint(array, pltpu.VMEM)
+DMA = pltpu.SemaphoreType.DMA
+MIB = 1024 * 1024
 
 
 def two_terms(values):
@@ -75,7 +81,19 @@
     )
 
 
-def frames_kernel(basis_ref, temporal_ref, spread_ref, inside_ref, out_ref, mix_ref):
+def frames_kernel(
+    basis_ref, temporal_hbm, spread_hbm, inside_hbm, out_ref,
+    temporal_ref, spread_ref, inside_ref, mix_ref, sems,
+):
+    copies = [
+        pltpu.make_async_copy(source, target, sems.at[i])
+        for i, (source, target) in enumerate(
+            [(temporal_hbm, temporal_ref), (spread_hbm, spread_ref), (inside_hbm, inside_ref)]
+        )
+    ]
+    for copy in copies:
+        copy.start()
+    copies[0].wait()
     first = lax.axis_index("grp") * GROUP
     frame = lax.broadcasted_iota(jnp.int32, (GROUP, GROUP * GROUP), 0) + first
     column = lax.broadcasted_iota(jnp.int32, (GROUP, GROUP * GROUP), 1)
@@ -86,9 +104,11 @@
     to_lane = lax.broadcasted_iota(jnp.int32, (2 * RANK, 2 * RANK), 1)
     apart = jnp.abs(from_lane - to_lane) == RANK
     swapped = dot(weights.astype(BF16), apart.astype(F32).astype(BF16))
+    copies[1].wait()
     signed = jnp.where(lane < RANK, weights, -weights)
     wide_re = dot(signed.astype(BF16), spread_ref[...])
     wide_im = dot(swapped.astype(BF16), spread_ref[...])
+    copies[2].wait()
     inside = inside_ref[...]
     for f in range(GROUP):
         block = jnp.concatenate(
@@ -108,53 +128,75 @@
     return pl.pallas_call(
         frames_kernel,
         out_shape=jax.ShapeDtypeStruct((GROUP, 72, 128), F32),
-        in_specs=[VMEM] * 4,
+        in_specs=[VMEM, HBM, HBM, HBM],
         out_specs=VMEM,
-        scratch_shapes=[pltpu.VMEM((GROUP * 48, rows), BF16)],
-        compiler_params=pltpu.CompilerParams(vmem_limit_bytes=24 * 1024 * 1024),
+        scratch_shapes=[
+            pltpu.VMEM((2 * RANK, GROUP * GROUP), BF16),
+            pltpu.VMEM((2 * RANK, rows), BF16),
+            pltpu.VMEM((2 * PART, rows), F32),
+            pltpu.VMEM((GROUP * 48, rows), BF16),
+            DMA((3,)),
+        ],
+        compiler_params=pltpu.CompilerParams(vmem_limit_bytes=12 * MIB),
         name="frames",
-    )(basis, temporal, spread, inside)
+    )(basis, *map(in_hbm, (temporal, spread, inside)))
 
 
 def data_kernel(
-    data_ref, lines_ref, dft_ref, temporal_ref, order_ref,
+    data_hbm, lines_hbm, dft_hbm, temporal_hbm, order_hbm,
     back_ref, ahead_ref, adjoint_ref, low_ref, weights_ref,
+    data_ref, lines_ref, dft_ref, temporal_ref, order_ref, data_sems, sems,
 ):
-    step = pl.program_id(0)
-
-    @pl.when(step == 0)
-    def tables():
-        places = lax.broadcasted_iota(jnp.int32, (N, LINES), 0)
-        chosen = (places == lines_ref[...]).astype(F32)
-        chosen_rows = chosen.T.astype(BF16)
-        chosen = chosen.astype(BF16)
-        for term in range(2):
-            cos_line = dot(chosen_rows, dft_ref[term])
-            sin_line = dot(chosen_rows, dft_ref[2 + term])
-            at = term * 96
-            ahead_ref[at : at + 96, 0:N] = jnp.concatenate([cos_line, -sin_line], 0).astype(BF16)
-            ahead_ref[at : at + 96, N : 2 * N] = jnp.concatenate([sin_line, cos_line], 0).astype(BF16)
-            cos_back = dot(dft_ref[term], chosen)
-            sin_back = dot(dft_ref[2 + term], chosen)
-            full = jnp.concatenate(
-                [
-                    jnp.concatenate([cos_back, -sin_back], 1),
-                    jnp.concatenate([sin_back, cos_back], 1),
-                ],
-                0,
-            ).astype(BF16)
-            if term == 0:
-                adjoint_ref[:, 0:96] = full
-                adjoint_ref[:, 96:192] = full
-            else:
-                low_ref[...] = full
-        weights_ref[...] = dot(order_ref[...], temporal_ref[...], (1, 1)).astype(BF16)
-
-    coils_here = data_ref.shape[2]
-    data_re = data_ref[0, 0].reshape(coils_here * 2 * LINES, N)
-    data_im = data_ref[0, 1].reshape(coils_here * 2 * LINES, N)
-    re_high, re_low = split(data_re)
-    im_high, im_low = split(data_im)
+    small = [
+        pltpu.make_async_copy(source, target, sems.at[i])
+        for i, (source, target) in enumerate(
+            [
+                (dft_hbm, dft_ref),
+                (lines_hbm, lines_ref),
+                (temporal_hbm, temporal_ref),
+                (order_hbm, order_ref),
+            ]
+        )
+    ]
+    chunks = [
+        pltpu.make_async_copy(
+            data_hbm.at[0, :, pl.ds(i * CHUNK, CHUNK)],
+            data_ref.at[:, pl.ds(i * CHUNK, CHUNK)],
+            data_sems.at[i],
+        )
+        for i in range(COILS // CHUNK)
+    ]
+    small[0].start()
+    small[1].start()
+    chunks[0].start()
+    for copy in small[2:] + chunks[1:]:
+        copy.start()
+    small[0].wait()
+    small[1].wait()
+    places = lax.broadcasted_iota(jnp.int32, (N, LINES), 0)
+    chosen = (places == lines_ref[...]).astype(F32)
+    chosen_rows = chosen.T.astype(BF16)
+    chosen = chosen.astype(BF16)
+    for term in range(2):
+        cos_line = dot(chosen_rows, dft_ref[term])
+        sin_line = dot(chosen_rows, dft_ref[2 + term])
+        at = term * 96
+        ahead_ref[at : at + 96, 0:N] = jnp.concatenate([cos_line, -sin_line], 0).astype(BF16)
+        ahead_ref[at : at + 96, N : 2 * N] = jnp.concatenate([sin_line, cos_line], 0).astype(BF16)
+        cos_back = dot(dft_ref[term], chosen)
+        sin_back = dot(dft_ref[2 + term], chosen)
+        full = jnp.concatenate(
+            [
+                jnp.concatenate([cos_back, -sin_back], 1),
+                jnp.concatenate([sin_back, cos_back], 1),
+            ],
+            0,
+        ).astype(BF16)
+        if term == 0:
+            adjoint_ref[:, 0:96] = full
+            adjoint_ref[:, 96:192] = full
+        else:
+            low_ref[...] = full
 
     def through(high, low, which):
         return (
@@ -163,48 +205,68 @@
             + dot(high, dft_ref[which + 1])
         )
 
-    back_re = through(re_high, re_low, 0) - through(im_high, im_low, 2)
-    back_im = through(re_high, re_low, 2) + through(im_high, im_low, 0)
-    back_ref[:, 0:LINES, :] = back_re.reshape(coils_here * 2, LINES, N)
-    back_ref[:, LINES : 2 * LINES, :] = back_im.reshape(coils_here * 2, LINES, N)
+    for i in range(COILS // CHUNK):
+        chunks[i].wait()
+        here = slice(i * CHUNK, (i + 1) * CHUNK)
+        re_high, re_low = split(data_ref[0, here].reshape(CHUNK * 2 * LINES, N))
+        im_high, im_low = split(data_ref[1, here].reshape(CHUNK * 2 * LINES, N))
+        back_re = through(re_high, re_low, 0) - through(im_high, im_low, 2)
+        back_im = through(re_high, re_low, 2) + through(im_high, im_low, 0)
+        pairs = slice(i * CHUNK * 2, (i + 1) * CHUNK * 2)
+        back_ref[pairs, 0:LINES, :] = back_re.reshape(CHUNK * 2, LINES, N)
+        back_ref[pairs, LINES : 2 * LINES, :] = back_im.reshape(CHUNK * 2, LINES, N)
+    small[2].wait()
+    small[3].wait()
+    weights_ref[...] = dot(order_ref[...], temporal_ref[...], (1, 1)).astype(BF16)
 
 
 def data_back(data, lines, dft, temporal, order):
-    coils_here = 4
-    whole = lambda *shape: pl.BlockSpec(shape, lambda i: (0,) * len(shape))
     return pl.pallas_call(
         data_kernel,
-        grid=(COILS // coils_here,),
         out_shape=(
-            jax.ShapeDtypeStruct((COILS * 2, 2 * LINES, N), F32),
-            jax.ShapeDtypeStruct((4 * LINES, 2 * N), BF16),
-            jax.ShapeDtypeStruct((2 * N, 4 * LINES), BF16),
-            jax.ShapeDtypeStruct((2 * N, 2 * LINES), BF16),
-            jax.ShapeDtypeStruct((GROUP * GROUP, 2 * RANK), BF16),
+            pltpu.VMEM((COILS * 2, 2 * LINES, N), F32),
+            pltpu.VMEM((4 * LINES, 2 * N), BF16),
+            pltpu.VMEM((2 * N, 4 * LINES), BF16),
+            pltpu.VMEM((2 * N, 2 * LINES), BF16),
+            pltpu.VMEM((GROUP * GROUP, 2 * RANK), BF16),
         ),
-        in_specs=[
-            pl.BlockSpec((1, 2, coils_here, 2, LINES, N), lambda i: (0, 0, i, 0, 0, 0)),
-            whole(1, LINES),
-            whole(4, N, N),
-            whole(2 * RANK, GROUP * GROUP),
-            whole(GROUP * GROUP, GROUP * GROUP),
+        in_specs=[HBM] * 5,
+        out_specs=(VMEM,) * 5,
+        scratch_shapes=[
+            pltpu.VMEM((2, COILS, 2, LINES, N), F32),
+            pltpu.VMEM((1, LINES), jnp.int32),
+            pltpu.VMEM((4, N, N), BF16),
+            pltpu.VMEM((2 * RANK, GROUP * GROUP), BF16),
+            pltpu.VMEM((GROUP * GROUP, GROUP * GROUP), BF16),
+            DMA((COILS // CHUNK,)),
+            DMA((4,)),
         ],
-        out_specs=(
-            pl.BlockSpec((coils_here * 2, 2 * LINES, N), lambda i: (i, 0, 0)),
-            whole(4 * LINES, 2 * N),
-            whole(2 * N, 4 * LINES),
-            whole(2 * N, 2 * LINES),
-            whole(GROUP * GROUP, 2 * RANK),
-        ),
-        compiler_params=pltpu.CompilerParams(vmem_limit_bytes=24 * 1024 * 1024),
+        compiler_params=pltpu.CompilerParams(vmem_limit_bytes=16 * MIB),
         name="data_back",
-    )(data, lines, dft, temporal, order)
+    )(*map(in_hbm, (data, lines, dft, temporal, order)))
 
 
 def model_kernel(
-    images_ref, coils_ref, back_ref, ahead_ref, adjoint_ref, low_ref,
-    depth_ref, lane_ref, out_ref, field_ref, grad_ref,
+    images_ref, coils_hbm, back_ref, ahead_ref, adjoint_ref, low_ref, depth_hbm, lane_hbm,
+    out_ref, coils_ref, depth_ref, lane_ref, field_ref, grad_ref, coil_sems, sems,
 ):
+    half = COILS // 2
+
+    def coil_copy(pos, side):
+        here = pl.ds(side * half, half)
+        return pltpu.make_async_copy(
+            coils_hbm.at[:, here, pos], coils_ref.at[pos, :, here], coil_sems.at[pos, side]
+        )
+
+    orders = [
+        pltpu.make_async_copy(depth_hbm, depth_ref, sems.at[0]),
+        pltpu.make_async_copy(lane_hbm, lane_ref, sems.at[1]),
+    ]
+    for pos in range(2):
+        for side in range(2):
+            coil_copy(pos, side).start()
+    for copy in orders:
+        copy.start()
     for d in range(GROUP):
         at = d * PART
         for part in range(2):
@@ -219,8 +281,8 @@
     for pos in range(2):
 
         def one_coil(coil, carry):
-            coil_re = coils_ref[0, coil, pos].astype(F32)
-            coil_im = coils_ref[1, coil, pos].astype(F32)
+            coil_re = coils_ref[pos, 0, coil].astype(F32)
+            coil_im = coils_ref[pos, 1, coil].astype(F32)
             field_re = field_ref[0, pos]
             field_im = field_ref[1, pos]
             re_high, re_low = split(coil_re * field_re - coil_im * field_im)
@@ -237,7 +299,11 @@
             grad_ref[1, pos] += coil_re * rows_im - coil_im * rows_re
             return carry
 
-        lax.fori_loop(0, COILS, one_coil, 0)
+        for side in range(2):
+            coil_copy(pos, side).wait()
+            lax.fori_loop(side * half, (side + 1) * half, one_coil, 0, unroll=True)
+    for copy in orders:
+        copy.wait()
     highs, lows = [], []
     for part in range(2):
         for pos in range(2):
@@ -259,15 +325,26 @@
     return pl.pallas_call(
         model_kernel,
         out_shape=jax.ShapeDtypeStruct((GROUP * GROUP, WIDE), F32),
-        in_specs=[VMEM] * 8,
+        in_specs=[VMEM, HBM, VMEM, VMEM, VMEM, VMEM, HBM, HBM],
         out_specs=VMEM,
         scratch_shapes=[
+            pltpu.VMEM((2, 2, COILS, N, N), BF16),
+            pltpu.VMEM((N, N), BF16),
+            pltpu.VMEM((4 * N, 4 * N), BF16),
             pltpu.VMEM((2, 2, N, N), F32),
             pltpu.VMEM((2, 2, N, N), F32),
+            DMA((2, 2)),
+            DMA((2,)),
         ],
-        compiler_params=pltpu.CompilerParams(vmem_limit_bytes=40 * 1024 * 1024),
+        compiler_params=pltpu.CompilerParams(vmem_limit_bytes=28 * MIB),
         name="model",
-    )(images, coils, back, ahead, adjoint, low, depth_order, lane_order)
+    )(
+        images,
+        in_hbm(coils),
+        *map(in_vmem, (back, ahead, adjoint, low)),
+        in_hbm(depth_order),
+        in_hbm(lane_order),
+    )
 
 
 def update_kernel(grads_ref, weights_ref, pick_ref, slab_ref, out_ref):
@@ -289,7 +366,7 @@
         out_shape=jax.ShapeDtypeStruct((2, 2 * PART * PART, RANK), F32),
         in_specs=[VMEM] * 4,
         out_specs=VMEM,
-        compiler_params=pltpu.CompilerParams(vmem_limit_bytes=16 * 1024 * 1024),
+        compiler_params=pltpu.CompilerParams(vmem_limit_bytes=16 * MIB),
         name="update",
     )(grads, weights, pick, slab)
 

time: 97.5 us -> 78.7 us (0.81)
  local copies, waits for them, and re-layouts: 20.8 us -> 5.87 us
  Pallas kernels: 31.4 us -> 24.7 us
  waiting for transfers between devices: 22.3 us -> 26.8 us
  starting transfers between devices: 20.4 us -> 19.1 us
    unnamed x41 -> x7, local copies, waits for them, and re-layouts: 16.5 us -> 1.58 us
    pallas_call x1, Pallas kernels: 23.6 us -> 15.1 us  [model(): pl.pallas_call(model_kernel, out_shape=jax.ShapeDtypeStruct((GROUP * GROU...]
    all_to_all x1, waiting for transfers between devices: 0.82 us -> 5.34 us  [on_device(): images = lax.all_to_all(sent, 'dev', 0, 0, tiled=True)]
    all_to_all x1, starting transfers between devices: 13.1 us -> 11.9 us  [on_device(): lax.all_to_all(sent.reshape(GROUP * GROUP, 1, WIDE), ('dev', 'grp'), 0, 0...]
    pallas_call x1, Pallas kernels: 3.86 us -> 4.88 us  [data_back(): pl.pallas_call(data_kernel, out_shape=(pltpu.VMEM((COILS * 2, 2 * LINES,...]
  transfers between devices with their start and end apart: 2 -> 2, of which waited for: 2 -> 2; matrix products, arithmetic and copies ran while one was open for 2% -> 3% of each run, Pallas kernels for 4% -> 6%
where the time goes in v1:
time: 78.7 us; the launch traced here: 78.3 us
  waiting for transfers between devices  26.8 us (34%)
  Pallas kernels  24.7 us (31%)
  starting transfers between devices  19.1 us (24%)
  local copies, waits for them, and re-layouts  5.87 us (7%)
  other arithmetic  1.65 us (2%)
    all_to_all x1, waiting for transfers between devices, on_device(): lax.all_to_all(sent.reshape(GROUP * GROUP, 1, WIDE), ('dev', 'grp'), 0, 0...  21.5 us
    pallas_call x1, Pallas kernels, model(): pl.pallas_call(model_kernel, out_shape=jax.ShapeDtypeStruct((GROUP * GROU...  15.1 us
    all_to_all x1, starting transfers between devices, on_device(): lax.all_to_all(sent.reshape(GROUP * GROUP, 1, WIDE), ('dev', 'grp'), 0, 0...  11.9 us
    all_to_all x1, starting transfers between devices, on_device(): images = lax.all_to_all(sent, 'dev', 0, 0, tiled=True)  7.23 us
    all_to_all x1, waiting for transfers between devices, on_device(): images = lax.all_to_all(sent, 'dev', 0, 0, tiled=True)  5.34 us
    pallas_call x1, Pallas kernels, data_back(): pl.pallas_call(data_kernel, out_shape=(pltpu.VMEM((COILS * 2, 2 * LINES,...  4.88 us
    pallas_call x1, Pallas kernels, frames(): pl.pallas_call(frames_kernel, out_shape=jax.ShapeDtypeStruct((GROUP, 72,...  2.89 us
    reshape x1, local copies, waits for them, and re-layouts, on_device(): flat_basis = jnp.transpose(spatial_basis, (0, 1, 3, 2, 4)).reshape(-1, N)  2.26 us
  transfers between devices with their start and end apart: 2, of which 2 were waited for; matrix products, arithmetic and copies ran while one was open for 3% of the time, Pallas kernels for 6%

profile of v1, /device:TPU:1, one launch (start us, length us, event | category | flops | bytes accessed | tf_op | source)
XLA Modules:
  0.0 78.3 jit_solution(2218717726391003677)
XLA Ops:
  0.0 2.3 %reshape.18.basis_ref = bf16[1536,192]{1,0:T(8,128)(2,1)S(1)} reshape(bf16[2,32,12,2,192]{4,3,2,1,0:T(2,128)(2,1)} %bitcast.15) | data formatting | bytes 1179648 | tf_op jit(solution)/shard_map/reshape | solution.py:377
  2.3 2.9 %frames.1 = f32[16,72,128]{2,1,0:T(8,128)} custom-call(bf16[1536,192]{1,0:T(8,128)(2,1)S(1)} %reshape.18.basis_ref, bf16[64,256]{1,0:T(8,128)(2,1)} %bitcast.16, bf16[64,1536]{1,0:T(8,128)(2,1)} %constant.26.clone.spread_hbm, f32[24,1536]{1,0:T(8,128)} %constant.27.clone.inside_hbm), custom_call_target="tpu_custom_call" | custom-call | tf_op jit(solution)/shard_map/frames/pallas_call | solution.py:128
  5.2 7.2 %all-to-all-start = ((f32[16,72,128]{2,1,0:T(8,128)}), f32[16,72,128]{2,1,0:T(8,128)}, u32[]{:S(2)}, u32[]{:S(2)}) async-start(f32[16,72,128]{2,1,0:T(8,128)} %frames.1), calls=%async_computation | async-start | bytes 1179648 | tf_op jit(solution)/shard_map/all_to_all | solution.py:379
  12.4 4.9 %data_back.1 = (f32[32,96,192]{2,1,0:T(8,128)S(1)}, bf16[192,384]{1,0:T(8,128)(2,1)S(1)}, bf16[384,192]{1,0:T(8,128)(2,1)S(1)}, bf16[384,96]{1,0:T(8,128)(2,1)S(1)}, bf16[256,64]{1,0:T(8,128)(2,1)S(1)}) custom-call(f32[1,2,16,2,48,192]{5,4,3,2,1,0:T(8,128)} %data_hbm.1, s32[1,48]{1,0:T(1,128)} %lines_hbm.1, bf16[4,192,192]{2,1,0:T(8,128)(2,1)} %constant.25.clone.dft_hbm, ...), custom_call_target="tpu_custom_call" | custom-call | tf_op jit(solution)/shard_map/data_back/pallas_call | solution.py:224
  17.3 0.0 copy-start.1
  17.3 0.6 copy-done.1
  17.9 5.3 %all-to-all-done.images_ref = f32[16,72,128]{2,1,0:T(8,128)} async-done(((f32[16,72,128]{2,1,0:T(8,128)}), f32[16,72,128]{2,1,0:T(8,128)}, u32[]{:S(2)}, u32[]{:S(2)}) %all-to-all-start) | async-done | bytes 589856 | tf_op jit(solution)/shard_map/all_to_all | solution.py:379
  23.3 0.0 copy-start.2
  23.3 0.9 %copy-done.2 = bf16[384,96]{1,0:T(8,128)(2,1)S(1)} copy-done((bf16[384,96]{1,0:T(8,128)(2,1)S(1)}, bf16[384,96]{1,0:T(8,128)(2,1)}, u32[]{:S(2)}) %copy-start.2) | copy-done | bytes 73752
  24.2 15.1 %model.1 = f32[256,640]{1,0:T(8,128)S(1)} custom-call(f32[16,72,128]{2,1,0:T(8,128)} %all-to-all-done.images_ref, bf16[2,16,2,192,192]{4,3,2,1,0:T(8,128)(2,1)} %coils_hbm.1, f32[32,96,192]{2,1,0:T(8,128)S(1)} %get-tuple-element.10.back_ref, bf16[192,384]{1,0:T(8,128)(2,1)S(1)} %get-tuple-element.11.ahead_ref, ...), custom_call_target="tpu_custom_call" | custom-call | tf_op jit(solution)/shard_map/model/pallas_call | solution.py:325
  39.2 0.0 copy-start
  39.2 1.5 %copy.15 = f32[256,1,640]{2,1,0:T(1,128)} copy(f32[256,1,640]{2,0,1:T(8,128)S(1)} %bitcast.12) | data formatting | bytes 1310720 | tf_op jit(solution)/shard_map/reshape | solution.py:387
  40.7 11.9 %all-to-all-start.1 = ((f32[256,1,640]{2,1,0:T(1,128)}), f32[256,1,640]{2,1,0:T(1,128)S(1)}, u32[]{:S(2)}, u32[]{:S(2)}) async-start(f32[256,1,640]{2,1,0:T(1,128)} %copy.15), calls=%async_computation.1 | async-start | bytes 1310720 | tf_op jit(solution)/shard_map/all_to_all | solution.py:386
  52.7 1.6 %convert_bitcast_fusion = f32[2,12,12,2,32]{2,3,1,4,0:T(2,128)S(1)} fusion(bf16[2,32,2,12,192]{4,2,3,1,0:T(2,128)(2,1)} %param.12, s32[]{:T(128)S(6)} %select_n.3), kind=kLoop, calls=%fused_computation | loop fusion | flops 18432 | bytes 110596 | tf_op jit(solution)/shard_map/convert_element_type | solution.py:390
  54.3 0.5 copy.16
  54.8 21.5 %all-to-all-done.1 = f32[256,1,640]{2,1,0:T(1,128)S(1)} async-done(((f32[256,1,640]{2,1,0:T(1,128)}), f32[256,1,640]{2,1,0:T(1,128)S(1)}, u32[]{:S(2)}, u32[]{:S(2)}) %all-to-all-start.1) | async-done | bytes 655392 | tf_op jit(solution)/shard_map/all_to_all | solution.py:386
  76.4 0.0 copy-done
  76.4 1.9 %update.1 = f32[2,288,32]{2,1,0:T(8,128)} custom-call(f32[256,640]{1,0:T(8,128)S(1)} %bitcast.13, bf16[256,64]{1,0:T(8,128)(2,1)S(1)} %get-tuple-element.14.weights_ref, bf16[2,288,640]{2,1,0:T(8,128)(2,1)S(1)} %copy-done, f32[2,288,32]{2,1,0:T(8,128)S(1)} %bitcast.14), custom_call_target="tpu_custom_call" | custom-call | tf_op jit(solution)/shard_map/update/pallas_call | solution.py:364
  (1 shorter events, 0.0 us)
Async XLA Ops:
  5.2 18.1 %all-to-all-start = ((f32[16,72,128]{2,1,0:T(8,128)}), f32[16,72,128]{2,1,0:T(8,128)}, u32[]{:S(2)}, u32[]{:S(2)}) async-start(f32[16,72,128]{2,1,0:T(8,128)} %frames.1), calls=%async_computation | async-start | bytes 1179648 | tf_op jit(solution)/shard_map/all_to_all | solution.py:379
  17.3 0.6 copy-start.1
  23.3 0.9 %copy-start.2 = (bf16[384,96]{1,0:T(8,128)(2,1)S(1)}, bf16[384,96]{1,0:T(8,128)(2,1)}, u32[]{:S(2)}) copy-start(bf16[384,96]{1,0:T(8,128)(2,1)} %copy-done.1) | copy-start | bytes 221188
  39.2 37.2 %copy-start = (bf16[2,288,640]{2,1,0:T(8,128)(2,1)S(1)}, bf16[2,288,640]{2,1,0:T(8,128)(2,1)}, u32[]{:S(2)}) copy-start(bf16[2,288,640]{2,1,0:T(8,128)(2,1)} %constant.31.clone.pick_ref) | copy-start | bytes 2211844
  40.7 35.6 %all-to-all-start.1 = ((f32[256,1,640]{2,1,0:T(1,128)}), f32[256,1,640]{2,1,0:T(1,128)S(1)}, u32[]{:S(2)}, u32[]{:S(2)}) async-start(f32[256,1,640]{2,1,0:T(1,128)} %copy.15), calls=%async_computation.1 | async-start | bytes 1310720 | tf_op jit(solution)/shard_map/all_to_all | solution.py:386

commit v2 on v1

v2 whole, which is shorter than its diff:
```python
import math

import jax
import jax.numpy as jnp
import numpy as np
from jax import lax
from jax.experimental import pallas as pl
from jax.experimental.pallas import tpu as pltpu
from jax.sharding import PartitionSpec as P

STEP_SIZE = 0.25
N = 192
PART = 12
RANK = 32
COILS = 16
LINES = 48
CHUNK = 4
GROUP = 16
VOX = 2 * PART * PART
WIDE = 384
STEPS = 8.0
TOP = 15.0
F32 = jnp.float32
BF16 = jnp.bfloat16
VMEM = pl.BlockSpec(memory_space=pltpu.VMEM)
HBM = pl.BlockSpec(memory_space=pltpu.HBM)
in_hbm = lambda array: pltpu.with_memory_space_constraint(array, pltpu.HBM)
in_vmem = lambda array: pltpu.with_memory_space_constraint(array, pltpu.VMEM)
DMA = pltpu.SemaphoreType.DMA
MIB = 1024 * 1024


def level_of(largest):
    return jnp.ceil(jnp.log2(jnp.maximum(largest, 1e-30)) * STEPS)


def scale_down(level):
    return jnp.exp2(TOP - level / STEPS)


def scale_up(level):
    return jnp.exp2(level / STEPS - TOP)


def pair_up(real, imag):
    real, imag = (
        jnp.clip(jnp.floor(part + 0.5), -32768.0, 32767.0).astype(jnp.int32)
        for part in (real, imag)
    )
    return jnp.bitwise_or(jnp.left_shift(real, 16), jnp.bitwise_and(imag, 65535))


def pair_apart(words):
    real = jnp.right_shift(words, 16)
    imag = jnp.right_shift(jnp.left_shift(words, 16), 16)
    return real.astype(F32), imag.astype(F32)


def two_terms(values):
    high = values.astype(np.float32).astype(jnp.bfloat16)
    low = (values - high.astype(np.float64)).astype(jnp.bfloat16)
    return high, low


def split(values):
    high = values.astype(BF16)
    return high, (values - high.astype(F32)).astype(BF16)


def dot(left, right, over=(1, 0)):
    return lax.dot_general(
        left, right, (((over[0],), (over[1],)), ((), ())), preferred_element_type=F32
    )


def constants():
    places = np.arange(N)
    angles = (places[:, None] * places[None, :] % N) * (2.0 * math.pi / N)
    cos_pair = two_terms(np.cos(angles) / math.sqrt(N))
    sin_pair = two_terms(np.sin(angles) / math.sqrt(N))
    dft = np.stack([*cos_pair, *sin_pair])
    columns = np.arange(2 * RANK * 2 * PART)
    spread = (columns[None, :] // (2 * PART) == np.arange(2 * RANK)[:, None])
    rows = np.arange(2 * PART)
    inside = (columns[None, :] % (2 * PART) == ((rows % PART) * 2 + rows // PART)[:, None])
    order = np.arange(N)
    depth_order = ((order % GROUP) * PART + order // GROUP)[:, None] == places[None, :]
    wide = np.arange(4 * N)
    target = (
        wide // (2 * N) * (2 * N)
        + wide // PART % GROUP * (2 * PART)
        + wide // N % 2 * PART
        + wide % PART
    )
    lane_order = target[:, None] == wide[None, :]
    peers = np.arange(GROUP * GROUP)
    frame_order = ((peers % GROUP) * GROUP + peers // GROUP)[:, None] == peers[None, :]
    out = np.arange(VOX)
    row, zz, pos = out // (2 * PART), out // 2 % PART, out % 2
    pick = (zz * 2 * PART + pos * PART + row)[:, None] == out[None, :]
    panel = np.arange(GROUP)[:, None] == np.arange(WIDE)[None, :] // (2 * PART)
    return dict(
        dft=dft,
        spread=spread.astype(jnp.bfloat16),
        inside=inside.astype(np.float32),
        depth_order=depth_order.astype(jnp.bfloat16),
        lane_order=lane_order.astype(jnp.bfloat16),
        frame_order=frame_order.astype(jnp.bfloat16),
        pick=pick.astype(jnp.bfloat16),
        panel=panel.astype(jnp.bfloat16),
    )


def frames_kernel(
    basis_ref, temporal_hbm, spread_hbm, inside_hbm, out_ref,
    temporal_ref, spread_ref, inside_ref, mix_ref, sems,
):
    copies = [
        pltpu.make_async_copy(source, target, sems.at[i])
        for i, (source, target) in enumerate(
            [(temporal_hbm, temporal_ref), (spread_hbm, spread_ref), (inside_hbm, inside_ref)]
        )
    ]
    for copy in copies:
        copy.start()
    copies[0].wait()
    first = lax.axis_index("grp") * GROUP
    frame = lax.broadcasted_iota(jnp.int32, (GROUP, GROUP * GROUP), 0) + first
    column = lax.broadcasted_iota(jnp.int32, (GROUP, GROUP * GROUP), 1)
    chosen = (frame == column).astype(F32).astype(BF16)
    weights = dot(chosen, temporal_ref[...], (1, 1))
    lane = lax.broadcasted_iota(jnp.int32, (GROUP, 2 * RANK), 1)
    from_lane = lax.broadcasted_iota(jnp.int32, (2 * RANK, 2 * RANK), 0)
    to_lane = lax.broadcasted_iota(jnp.int32, (2 * RANK, 2 * RANK), 1)
    apart = jnp.abs(from_lane - to_lane) == RANK
    swapped = dot(weights.astype(BF16), apart.astype(F32).astype(BF16))
    copies[1].wait()
    signed = jnp.where(lane < RANK, weights, -weights)
    wide_re = dot(signed.astype(BF16), spread_ref[...])
    wide_im = dot(swapped.astype(BF16), spread_ref[...])
    copies[2].wait()
    inside = inside_ref[...]
    for f in range(GROUP):
        block = jnp.concatenate(
            [inside * wide_re[f : f + 1], inside * wide_im[f : f + 1]], axis=0
        )
        mix_ref[f * 48 : (f + 1) * 48, :] = block.astype(BF16)
    images = dot(mix_ref[...], basis_ref[...])
    for f in range(GROUP):
        image = images[f * 48 : (f + 1) * 48]
        largest = jnp.max(jnp.max(jnp.abs(image), axis=0, keepdims=True), axis=1, keepdims=True)
        level = level_of(largest)
        image = image * scale_down(level)
        words = pair_up(image[0:24], image[24:48])
        words = jnp.concatenate([words[0:PART], words[PART : 2 * PART]], 1)
        for block in range(3):
            out_ref[f, block * PART : (block + 1) * PART, :] = words[
                :, block * 128 : (block + 1) * 128
            ]
        out_ref[f, 36:40, :] = jnp.broadcast_to(level, (4, 128)).astype(jnp.int32)


def frames(basis, temporal, spread, inside):
    rows = 2 * RANK * 2 * PART
    return pl.pallas_call(
        frames_kernel,
        out_shape=jax.ShapeDtypeStruct((GROUP, 40, 128), jnp.int32),
        in_specs=[VMEM, HBM, HBM, HBM],
        out_specs=VMEM,
        scratch_shapes=[
            pltpu.VMEM((2 * RANK, GROUP * GROUP), BF16),
            pltpu.VMEM((2 * RANK, rows), BF16),
            pltpu.VMEM((2 * PART, rows), F32),
            pltpu.VMEM((GROUP * 48, rows), BF16),
            DMA((3,)),
        ],
        compiler_params=pltpu.CompilerParams(vmem_limit_bytes=12 * MIB),
        name="frames",
    )(basis, *map(in_hbm, (temporal, spread, inside)))


def data_kernel(
    data_hbm, lines_hbm, dft_hbm, temporal_hbm, order_hbm,
    back_ref, ahead_ref, adjoint_ref, weights_ref,
    data_ref, lines_ref, dft_ref, temporal_ref, order_ref, data_sems, sems,
):
    small = [
        pltpu.make_async_copy(source, target, sems.at[i])
        for i, (source, target) in enumerate(
            [
                (dft_hbm, dft_ref),
                (lines_hbm, lines_ref),
                (temporal_hbm, temporal_ref),
                (order_hbm, order_ref),
            ]
        )
    ]
    chunks = [
        pltpu.make_async_copy(
            data_hbm.at[0, :, pl.ds(i * CHUNK, CHUNK)],
            data_ref.at[:, pl.ds(i * CHUNK, CHUNK)],
            data_sems.at[i],
        )
        for i in range(COILS // CHUNK)
    ]
    small[0].start()
    small[1].start()
    chunks[0].start()
    for copy in small[2:] + chunks[1:]:
        copy.start()
    small[0].wait()
    small[1].wait()
    places = lax.broadcasted_iota(jnp.int32, (N, LINES), 0)
    chosen = (places == lines_ref[...]).astype(F32)
    chosen_rows = chosen.T.astype(BF16)
    chosen = chosen.astype(BF16)
    for term in range(2):
        cos_line = dot(chosen_rows, dft_ref[term])
        sin_line = dot(chosen_rows, dft_ref[2 + term])
        from_re = jnp.concatenate([cos_line, -sin_line], 0).astype(BF16)
        from_im = jnp.concatenate([sin_line, cos_line], 0).astype(BF16)
        at = term * 96
        ahead_ref[at : at + 96, 0:N] = jnp.concatenate([cos_line, -sin_line], 0).astype(BF16)
        ahead_ref[at : at + 96, N : 2 * N] = jnp.concatenate([sin_line, cos_line], 0).astype(BF16)
        cos_back = dot(dft_ref[term], chosen)
        sin_back = dot(dft_ref[2 + term], chosen)
        adjoint_ref[0:N, at : at + 48] = cos_back.astype(BF16)
        adjoint_ref[0:N, at + 48 : at + 96] = (-sin_back).astype(BF16)
        adjoint_ref[N : 2 * N, at : at + 48] = sin_back.astype(BF16)
        adjoint_ref[N : 2 * N, at + 48 : at + 96] = cos_back.astype(BF16)

    def through(high, low, which):
        return (
            dot(high, dft_ref[which])
            + dot(low, dft_ref[which])
            + dot(high, dft_ref[which + 1])
        )

    for i in range(COILS // CHUNK):
        chunks[i].wait()
        here = slice(i * CHUNK, (i + 1) * CHUNK)
        re_high, re_low = split(data_ref[0, here].reshape(CHUNK * 2 * LINES, N))
        im_high, im_low = split(data_ref[1, here].reshape(CHUNK * 2 * LINES, N))
        back_re = through(re_high, re_low, 0) - through(im_high, im_low, 2)
        back_im = through(re_high, re_low, 2) + through(im_high, im_low, 0)
        for part, values in enumerate((back_re, back_im)):
            values = values.reshape(CHUNK, 2, LINES, N)
            at = slice(part * LINES, (part + 1) * LINES)
            for pos in range(2):
                back_ref[here, at, pos * N : (pos + 1) * N] = values[:, pos]
    small[2].wait()
    small[3].wait()
    weights = dot(order_ref[...], temporal_ref[...], (1, 1)).astype(BF16)
    peers = GROUP * GROUP
    weights_ref[0:peers, 0:RANK] = weights[:, 0:RANK]
    weights_ref[0:peers, RANK : 2 * RANK] = -weights[:, RANK : 2 * RANK]
    weights_ref[peers : 2 * peers, 0:RANK] = weights[:, RANK : 2 * RANK]
    weights_ref[peers : 2 * peers, RANK : 2 * RANK] = weights[:, 0:RANK]


def data_back(data, lines, dft, temporal, order):
    return pl.pallas_call(
        data_kernel,
        out_shape=(
            pltpu.VMEM((COILS, 2 * LINES, 2 * N), F32),
            pltpu.VMEM((4 * LINES, 2 * N), BF16),
            pltpu.VMEM((2 * N, 4 * LINES), BF16),
            jax.ShapeDtypeStruct((2 * GROUP * GROUP, 2 * RANK), BF16),
        ),
        in_specs=[HBM] * 5,
        out_specs=(VMEM,) * 4,
        scratch_shapes=[
            pltpu.VMEM((2, COILS, 2, LINES, N), F32),
            pltpu.VMEM((1, LINES), jnp.int32),
            pltpu.VMEM((4, N, N), BF16),
            pltpu.VMEM((2 * RANK, GROUP * GROUP), BF16),
            pltpu.VMEM((GROUP * GROUP, GROUP * GROUP), BF16),
            DMA((COILS // CHUNK,)),
            DMA((4,)),
        ],
        compiler_params=pltpu.CompilerParams(vmem_limit_bytes=16 * MIB),
        name="data_back",
    )(*map(in_hbm, (data, lines, dft, temporal, order)))


def model_kernel(
    images_ref, back_ref, ahead_ref, adjoint_ref, coils_hbm, depth_hbm, lane_hbm, panel_hbm,
    out_ref, coils_ref, depth_ref, lane_ref, panel_ref, field_ref, grad_ref,
    lines_ref, rows_ref, coil_sems, sems,
):
    def coil_copy(coil, part):
        return pltpu.make_async_copy(
            coils_hbm.at[part, coil], coils_ref.at[part, coil], coil_sems.at[part, coil]
        )

    for coil in range(COILS):
        for part in range(2):
            coil_copy(coil, part).start()
    orders = [
        pltpu.make_async_copy(source, target, sems.at[i])
        for i, (source, target) in enumerate(
            [(depth_hbm, depth_ref), (lane_hbm, lane_ref), (panel_hbm, panel_ref)]
        )
    ]
    for copy in orders:
        copy.start()
    for d in range(GROUP):
        here = slice(d * PART, (d + 1) * PART)
        words = images_ref[d]
        scale = scale_up(words[36:37].astype(F32))
        for part, values in enumerate(pair_apart(words[0:36])):
            values = values * scale
            for block in range(3):
                field_ref[part, here, block * 128 : (block + 1) * 128] = values[
                    block * PART : (block + 1) * PART
                ]
    grad_ref[...] = jnp.zeros_like(grad_ref)
    lines_ref[:, 0 : 2 * N] = ahead_ref[...]
    lines_ref[0:96, 2 * N : 4 * N] = ahead_ref[0:96, :]
    lines_ref[96:192, 2 * N : 4 * N] = jnp.zeros((96, 2 * N), BF16)
    rows_ref[:, 0:96] = adjoint_ref[:, 0:96]
    rows_ref[:, 96:192] = adjoint_ref[:, 0:96]
    rows_ref[:, 192:288] = adjoint_ref[:, 96:192]

    def one_coil(coil):
        coil_re, coil_im = (
            jnp.concatenate([coils_ref[part, coil, 0], coils_ref[part, coil, 1]], 1).astype(F32)
            for part in range(2)
        )
        field_re, field_im = field_ref[0], field_ref[1]
        re_high, re_low = split(coil_re * field_re - coil_im * field_im)
        im_high, im_low = split(coil_re * field_im + coil_im * field_re)
        first = dot(lines_ref[...], jnp.concatenate([re_high, im_high, re_low, im_low], 0))
        high, low = split(first[0:96] + first[96:192] - back_ref[coil])
        rows = dot(rows_ref[...], jnp.concatenate([high, low, high], 0))
        rows_re, rows_im = rows[0:N], rows[N : 2 * N]
        grad_ref[0] += coil_re * rows_re + coil_im * rows_im
        grad_ref[1] += coil_re * rows_im - coil_im * rows_re

    def some_coils(step, carry):
        for i in range(CHUNK):
            for part in range(2):
                coil_copy(step * CHUNK + i, part).wait()
        for i in range(CHUNK):
            one_coil(step * CHUNK + i)
        return carry

    lax.fori_loop(0, COILS // CHUNK, some_coils, 0)
    for copy in orders:
        copy.wait()
    total = jnp.zeros((N, 4 * N), F32)
    for channel in range(4):
        order = lane_ref[channel * N : (channel + 1) * N, :]
        for term in split(grad_ref[channel // 2, :, channel % 2 * N : (channel % 2 + 1) * N]):
            total = total + dot(dot(depth_ref[...], term, (1, 1)).astype(BF16), order)
    real = total[:, 0:WIDE].reshape(PART, GROUP, WIDE)
    imag = total[:, WIDE : 2 * WIDE].reshape(PART, GROUP, WIDE)
    largest = jnp.max(jnp.maximum(jnp.abs(real), jnp.abs(imag)), axis=0)
    largest = jnp.max(largest.T.reshape(GROUP, 2 * PART, GROUP), axis=1)
    level = level_of(largest).T
    high, low = split(level)
    level = dot(high, panel_ref[...]) + dot(low, panel_ref[...])
    scale = scale_down(level)[None]
    words = pair_up(real * scale, imag * scale)
    level = level.astype(jnp.int32)
    for d in range(GROUP):
        lanes = slice(d * 2 * PART, (d + 1) * 2 * PART)
        pieces = [words[zz, :, lanes] for zz in range(PART)]
        pieces += [level[:, lanes]] * (WIDE // (2 * PART) - PART)
        out_ref[d * GROUP : (d + 1) * GROUP, 0, :] = jnp.concatenate(pieces, 1)


def model(images, back, ahead, adjoint, coils, depth_order, lane_order, panel):
    return pl.pallas_call(
        model_kernel,
        out_shape=jax.ShapeDtypeStruct((GROUP * GROUP, 1, WIDE), jnp.int32),
        in_specs=[VMEM] * 4 + [HBM] * 4,
        out_specs=VMEM,
        scratch_shapes=[
            pltpu.VMEM((2, COILS, 2, N, N), BF16),
            pltpu.VMEM((N, N), BF16),
            pltpu.VMEM((4 * N, 4 * N), BF16),
            pltpu.VMEM((GROUP, WIDE), BF16),
            pltpu.VMEM((2, N, 2 * N), F32),
            pltpu.VMEM((2, N, 2 * N), F32),
            pltpu.VMEM((4 * LINES, 4 * N), BF16),
            pltpu.VMEM((2 * N, 6 * LINES), BF16),
            DMA((2, COILS)),
            DMA((3,)),
        ],
        compiler_params=pltpu.CompilerParams(vmem_limit_bytes=24 * MIB),
        name="model",
    )(
        images,
        *map(in_vmem, (back, ahead, adjoint)),
        *map(in_hbm, (coils, depth_order, lane_order, panel)),
    )


def update_kernel(grads_ref, weights_ref, pick_ref, slab_ref, out_ref):
    words = grads_ref[:, 0, :].T
    scale = scale_up(words[VOX : VOX + 1].astype(F32))
    real, imag = pair_apart(words[0:VOX])
    high, low = split(jnp.concatenate([real * scale, imag * scale], 1))
    grad = dot(high, weights_ref[...]) + dot(low, weights_ref[...])
    high, low = split(grad)
    grad = dot(pick_ref[...], high) + dot(pick_ref[...], low)
    out_ref[0] = slab_ref[0] - STEP_SIZE * grad[:, 0:RANK]
    out_ref[1] = slab_ref[1] - STEP_SIZE * grad[:, RANK : 2 * RANK]


def update(grads, weights, pick, slab):
    return pl.pallas_call(
        update_kernel,
        out_shape=jax.ShapeDtypeStruct((2, 2 * PART * PART, RANK), F32),
        in_specs=[VMEM] * 4,
        out_specs=VMEM,
        compiler_params=pltpu.CompilerParams(vmem_limit_bytes=16 * MIB),
        name="update",
    )(grads, weights, pick, slab)


def on_device(spatial_basis, temporal, coil_maps, kspace_data, sampled_lines):
    table = {name: jnp.asarray(value) for name, value in constants().items()}
    flat_temporal = temporal.reshape(2 * RANK, GROUP * GROUP)
    flat_basis = jnp.transpose(spatial_basis, (0, 1, 3, 2, 4)).reshape(-1, N)
    sent = frames(flat_basis, flat_temporal, table["spread"], table["inside"])
    images = lax.all_to_all(sent, "dev", 0, 0, tiled=True)
    back, ahead, adjoint, weights = data_back(
        kspace_data, sampled_lines, table["dft"], flat_temporal, table["frame_order"]
    )
    sent = model(
        images, back, ahead, adjoint, coil_maps,
        table["depth_order"], table["lane_order"], table["panel"],
    )
    grads = lax.all_to_all(sent, ("dev", "grp"), 0, 0, tiled=True)
    slab = lax.dynamic_slice_in_dim(spatial_basis, lax.axis_index("grp") * PART, PART, 4)
    slab = jnp.transpose(slab, (0, 3, 4, 2, 1)).reshape(2, 2 * PART * PART, RANK).astype(F32)
    result = update(grads, weights, table["pick"], slab)
    return jnp.transpose(result.reshape(2, PART, PART, 2, RANK), (0, 4, 3, 1, 2))


def solution(mesh):
    placed = (
        P(None, None, None, "dev", None),
        P(),
        P(),
        P(("grp", "dev"), None, None, None, None, None),
        P(("grp", "dev"), None),
    )
    return jax.shard_map(
        on_device,
        mesh=mesh,
        in_specs=placed,
        out_specs=P(None, None, None, "dev", "grp"),
        check_vma=False,
    )
```

time: 78.7 us -> 68.1 us (0.87)
  waiting for transfers between devices: 26.8 us -> 18.5 us
  local copies, waits for them, and re-layouts: 5.87 us -> 2.78 us
    all_to_all x1, waiting for transfers between devices: 21.5 us -> 16.2 us  [on_device(): grads = lax.all_to_all(sent, ('dev', 'grp'), 0, 0, tiled=True)]
    all_to_all x1, waiting for transfers between devices: 5.34 us -> 2.27 us  [on_device(): images = lax.all_to_all(sent, 'dev', 0, 0, tiled=True)]
    unnamed x7 -> x2, local copies, waits for them, and re-layouts: 1.58 us -> 0.01 us
    reshape x1 -> x0, local copies, waits for them, and re-layouts: 1.51 us -> none  [on_device(): sent.reshape(GROUP * GROUP, 1, WIDE)]
    all_to_all x1, starting transfers between devices: 11.9 us -> 12.7 us  [on_device(): grads = lax.all_to_all(sent, ('dev', 'grp'), 0, 0, tiled=True)]
  transfers between devices with their start and end apart: 2 -> 2, of which waited for: 2 -> 2; matrix products, arithmetic and copies ran while one was open for 3% -> 3% of each run, Pallas kernels for 6% -> 8%
where the time goes in v2:
time: 68.1 us; the launch traced here: 67.8 us
  Pallas kernels  25.2 us (37%)
  starting transfers between devices  19.6 us (29%)
  waiting for transfers between devices  18.5 us (27%)
  local copies, waits for them, and re-layouts  2.78 us (4%)
  other arithmetic  1.65 us (2%)
    all_to_all x1, waiting for transfers between devices, on_device(): grads = lax.all_to_all(sent, ('dev', 'grp'), 0, 0, tiled=True)  16.2 us
    pallas_call x1, Pallas kernels, model(): pl.pallas_call(model_kernel, out_shape=jax.ShapeDtypeStruct((GROUP * GROU...  15.1 us
    all_to_all x1, starting transfers between devices, on_device(): grads = lax.all_to_all(sent, ('dev', 'grp'), 0, 0, tiled=True)  12.7 us
    all_to_all x1, starting transfers between devices, on_device(): images = lax.all_to_all(sent, 'dev', 0, 0, tiled=True)  6.84 us
    pallas_call x1, Pallas kernels, data_back(): pl.pallas_call(data_kernel, out_shape=(pltpu.VMEM((COILS, 2 * LINES, 2 *...  5.33 us
    pallas_call x1, Pallas kernels, frames(): pl.pallas_call(frames_kernel, out_shape=jax.ShapeDtypeStruct((GROUP, 40,...  3.03 us
    all_to_all x1, waiting for transfers between devices, on_device(): images = lax.all_to_all(sent, 'dev', 0, 0, tiled=True)  2.27 us
    reshape x1, local copies, waits for them, and re-layouts, on_device(): flat_basis = jnp.transpose(spatial_basis, (0, 1, 3, 2, 4)).reshape(-1, N)  2.26 us
  transfers between devices with their start and end apart: 2, of which 2 were waited for; matrix products, arithmetic and copies ran while one was open for 3% of the time, Pallas kernels for 8%

profile of v2, /device:TPU:1, one launch (start us, length us, event | category | flops | bytes accessed | tf_op | source)
XLA Modules:
  0.0 67.8 jit_solution(875847794604695026)
XLA Ops:
  0.0 2.3 %reshape.12.basis_ref = bf16[1536,192]{1,0:T(8,128)(2,1)S(1)} reshape(bf16[2,32,12,2,192]{4,3,2,1,0:T(2,128)(2,1)} %bitcast.9) | data formatting | bytes 1179648 | tf_op jit(solution)/shard_map/reshape | solution.py:426
  2.3 3.0 %frames.1 = s32[16,40,128]{2,1,0:T(8,128)} custom-call(bf16[1536,192]{1,0:T(8,128)(2,1)S(1)} %reshape.12.basis_ref, bf16[64,256]{1,0:T(8,128)(2,1)} %bitcast.10, bf16[64,1536]{1,0:T(8,128)(2,1)} %constant.28.clone.spread_hbm, f32[24,1536]{1,0:T(8,128)} %constant.29.clone.inside_hbm), custom_call_target="tpu_custom_call" | custom-call | tf_op jit(solution)/shard_map/frames/pallas_call | solution.py:165
  5.3 6.8 %all-to-all-start = ((s32[16,40,128]{2,1,0:T(8,128)}), s32[16,40,128]{2,1,0:T(8,128)S(1)}, u32[]{:S(2)}, u32[]{:S(2)}) async-start(s32[16,40,128]{2,1,0:T(8,128)} %frames.1), calls=%async_computation | async-start | bytes 655360 | tf_op jit(solution)/shard_map/all_to_all | solution.py:428
  12.1 5.3 %data_back.1 = (f32[16,96,384]{2,1,0:T(8,128)S(1)}, bf16[192,384]{1,0:T(8,128)(2,1)S(1)}, bf16[384,192]{1,0:T(8,128)(2,1)S(1)}, bf16[512,64]{1,0:T(8,128)(2,1)S(1)}) custom-call(f32[1,2,16,2,48,192]{5,4,3,2,1,0:T(8,128)} %data_hbm.1, s32[1,48]{1,0:T(1,128)} %lines_hbm.1, bf16[4,192,192]{2,1,0:T(8,128)(2,1)} %constant.27.clone.dft_hbm, ...), custom_call_target="tpu_custom_call" | custom-call | tf_op jit(solution)/shard_map/data_back/pallas_call | solution.py:262
  17.5 2.3 %all-to-all-done.images_ref = s32[16,40,128]{2,1,0:T(8,128)S(1)} async-done(((s32[16,40,128]{2,1,0:T(8,128)}), s32[16,40,128]{2,1,0:T(8,128)S(1)}, u32[]{:S(2)}, u32[]{:S(2)}) %all-to-all-start) | async-done | bytes 327712 | tf_op jit(solution)/shard_map/all_to_all | solution.py:428
  19.8 15.1 %model.1 = s32[256,1,384]{2,1,0:T(1,128)} custom-call(s32[16,40,128]{2,1,0:T(8,128)S(1)} %all-to-all-done.images_ref, f32[16,96,384]{2,1,0:T(8,128)S(1)} %get-tuple-element.9.back_ref, bf16[192,384]{1,0:T(8,128)(2,1)S(1)} %get-tuple-element.10.ahead_ref, bf16[384,192]{1,0:T(8,128)(2,1)S(1)} %get-tuple-element.11.adjoint_ref, ...), custom_call_target="tpu_custom_call" | custom-call | tf_op jit(solution)/shard_map/model/pallas_call | solution.py:374
  34.9 0.0 copy-start
  34.9 12.7 %all-to-all-start.1 = ((s32[256,1,384]{2,1,0:T(1,128)}), s32[256,1,384]{2,1,0:T(1,128)S(1)}, u32[]{:S(2)}, u32[]{:S(2)}) async-start(s32[256,1,384]{2,1,0:T(1,128)} %model.1), calls=%async_computation.1 | async-start | bytes 786432 | tf_op jit(solution)/shard_map/all_to_all | solution.py:436
  47.7 1.6 %convert_bitcast_fusion = f32[2,12,12,2,32]{2,3,1,4,0:T(2,128)S(1)} fusion(bf16[2,32,2,12,192]{4,2,3,1,0:T(2,128)(2,1)} %param.13, s32[]{:T(128)S(6)} %select_n.3), kind=kLoop, calls=%fused_computation | loop fusion | flops 18432 | bytes 110596 | tf_op jit(solution)/shard_map/convert_element_type | solution.py:438
  49.3 0.5 copy.15
  49.8 16.2 %all-to-all-done.1.grads_ref = s32[256,1,384]{2,1,0:T(1,128)S(1)} async-done(((s32[256,1,384]{2,1,0:T(1,128)}), s32[256,1,384]{2,1,0:T(1,128)S(1)}, u32[]{:S(2)}, u32[]{:S(2)}) %all-to-all-start.1) | async-done | bytes 393248 | tf_op jit(solution)/shard_map/all_to_all | solution.py:436
  66.1 0.0 copy-done
  66.1 1.7 %update.1 = f32[2,288,32]{2,1,0:T(8,128)} custom-call(s32[256,1,384]{2,1,0:T(1,128)S(1)} %all-to-all-done.1.grads_ref, bf16[512,64]{1,0:T(8,128)(2,1)S(1)} %get-tuple-element.12.weights_ref, bf16[288,288]{1,0:T(8,128)(2,1)S(1)} %copy-done, f32[2,288,32]{2,1,0:T(8,128)S(1)} %bitcast.8), custom_call_target="tpu_custom_call" | custom-call | tf_op jit(solution)/shard_map/update/pallas_call | solution.py:413
Async XLA Ops:
  5.3 14.5 %all-to-all-start = ((s32[16,40,128]{2,1,0:T(8,128)}), s32[16,40,128]{2,1,0:T(8,128)S(1)}, u32[]{:S(2)}, u32[]{:S(2)}) async-start(s32[16,40,128]{2,1,0:T(8,128)} %frames.1), calls=%async_computation | async-start | bytes 655360 | tf_op jit(solution)/shard_map/all_to_all | solution.py:428
  34.9 31.2 %copy-start = (bf16[288,288]{1,0:T(8,128)(2,1)S(1)}, bf16[288,288]{1,0:T(8,128)(2,1)}, u32[]{:S(2)}) copy-start(bf16[288,288]{1,0:T(8,128)(2,1)} %constant.33.clone.pick_ref) | copy-start | bytes 497668
  34.9 31.2 %all-to-all-start.1 = ((s32[256,1,384]{2,1,0:T(1,128)}), s32[256,1,384]{2,1,0:T(1,128)S(1)}, u32[]{:S(2)}, u32[]{:S(2)}) async-start(s32[256,1,384]{2,1,0:T(1,128)} %model.1), calls=%async_computation.1 | async-start | bytes 786432 | tf_op jit(solution)/shard_map/all_to_all | solution.py:436

commit v3 on v2

--- a/solution.py
+++ b/solution.py
@@ -1,3 +1,4 @@
+import functools
 import math
 
 import jax
@@ -14,7 +15,10 @@
 RANK = 32
 COILS = 16
 LINES = 48
+EARLY = 1
+GROUPS = [range(1, 3), range(3, 6), range(6, 11), range(11, 16)]
 CHUNK = 4
+TOGETHER = 15
 GROUP = 16
 VOX = 2 * PART * PART
 WIDE = 384
@@ -85,26 +89,17 @@
     inside = (columns[None, :] % (2 * PART) == ((rows % PART) * 2 + rows // PART)[:, None])
     order = np.arange(N)
     depth_order = ((order % GROUP) * PART + order // GROUP)[:, None] == places[None, :]
-    wide = np.arange(4 * N)
-    target = (
-        wide // (2 * N) * (2 * N)
-        + wide // PART % GROUP * (2 * PART)
-        + wide // N % 2 * PART
-        + wide % PART
-    )
-    lane_order = target[:, None] == wide[None, :]
     peers = np.arange(GROUP * GROUP)
     frame_order = ((peers % GROUP) * GROUP + peers // GROUP)[:, None] == peers[None, :]
     out = np.arange(VOX)
     row, zz, pos = out // (2 * PART), out // 2 % PART, out % 2
     pick = (zz * 2 * PART + pos * PART + row)[:, None] == out[None, :]
-    panel = np.arange(GROUP)[:, None] == np.arange(WIDE)[None, :] // (2 * PART)
+    panel = places[:, None] == places[None, :] // PART * PART
     return dict(
         dft=dft,
         spread=spread.astype(jnp.bfloat16),
         inside=inside.astype(np.float32),
         depth_order=depth_order.astype(jnp.bfloat16),
-        lane_order=lane_order.astype(jnp.bfloat16),
         frame_order=frame_order.astype(jnp.bfloat16),
         pick=pick.astype(jnp.bfloat16),
         panel=panel.astype(jnp.bfloat16),
@@ -112,13 +107,18 @@
 
 
 def frames_kernel(
-    basis_ref, temporal_hbm, spread_hbm, inside_hbm, out_ref,
-    temporal_ref, spread_ref, inside_ref, mix_ref, sems,
+    basis_hbm, temporal_hbm, spread_hbm, inside_hbm, out_ref,
+    basis_ref, temporal_ref, spread_ref, inside_ref, mix_ref, sems,
 ):
     copies = [
         pltpu.make_async_copy(source, target, sems.at[i])
         for i, (source, target) in enumerate(
-            [(temporal_hbm, temporal_ref), (spread_hbm, spread_ref), (inside_hbm, inside_ref)]
+            [
+                (temporal_hbm, temporal_ref),
+                (spread_hbm, spread_ref),
+                (inside_hbm, inside_ref),
+                (basis_hbm, basis_ref),
+            ]
         )
     ]
     for copy in copies:
@@ -145,7 +145,9 @@
             [inside * wide_re[f : f + 1], inside * wide_im[f : f + 1]], axis=0
         )
         mix_ref[f * 48 : (f + 1) * 48, :] = block.astype(BF16)
-    images = dot(mix_ref[...], basis_ref[...])
+    copies[3].wait()
+    basis = basis_ref[...].reshape(2 * RANK * 2 * PART, N)
+    images = dot(mix_ref[...], basis)
     for f in range(GROUP):
         image = images[f * 48 : (f + 1) * 48]
         largest = jnp.max(jnp.max(jnp.abs(image), axis=0, keepdims=True), axis=1, keepdims=True)
@@ -165,23 +167,24 @@
     return pl.pallas_call(
         frames_kernel,
         out_shape=jax.ShapeDtypeStruct((GROUP, 40, 128), jnp.int32),
-        in_specs=[VMEM, HBM, HBM, HBM],
+        in_specs=[HBM] * 4,
         out_specs=VMEM,
         scratch_shapes=[
+            pltpu.VMEM((rows // 2, 2, N), BF16),
             pltpu.VMEM((2 * RANK, GROUP * GROUP), BF16),
             pltpu.VMEM((2 * RANK, rows), BF16),
             pltpu.VMEM((2 * PART, rows), F32),
             pltpu.VMEM((GROUP * 48, rows), BF16),
-            DMA((3,)),
+            DMA((4,)),
         ],
-        compiler_params=pltpu.CompilerParams(vmem_limit_bytes=12 * MIB),
+        compiler_params=pltpu.CompilerParams(vmem_limit_bytes=16 * MIB),
         name="frames",
-    )(basis, *map(in_hbm, (temporal, spread, inside)))
+    )(*map(in_hbm, (basis, temporal, spread, inside)))
 
 
 def data_kernel(
-    data_hbm, lines_hbm, dft_hbm, temporal_hbm, order_hbm,
-    back_ref, ahead_ref, adjoint_ref, weights_ref,
+    data_hbm, coils_hbm, lines_hbm, dft_hbm, temporal_hbm, order_hbm,
+    back_ref, early_ref, ahead_ref, adjoint_ref, weights_ref,
     data_ref, lines_ref, dft_ref, temporal_ref, order_ref, data_sems, sems,
 ):
     small = [
@@ -192,6 +195,7 @@
                 (lines_hbm, lines_ref),
                 (temporal_hbm, temporal_ref),
                 (order_hbm, order_ref),
+                (coils_hbm.at[:, pl.ds(0, EARLY)], early_ref),
             ]
         )
     ]
@@ -250,6 +254,7 @@
                 back_ref[here, at, pos * N : (pos + 1) * N] = values[:, pos]
     small[2].wait()
     small[3].wait()
+    small[4].wait()
     weights = dot(order_ref[...], temporal_ref[...], (1, 1)).astype(BF16)
     peers = GROUP * GROUP
     weights_ref[0:peers, 0:RANK] = weights[:, 0:RANK]
@@ -258,17 +263,18 @@
     weights_ref[peers : 2 * peers, RANK : 2 * RANK] = weights[:, 0:RANK]
 
 
-def data_back(data, lines, dft, temporal, order):
+def data_back(data, coils, lines, dft, temporal, order):
     return pl.pallas_call(
         data_kernel,
         out_shape=(
             pltpu.VMEM((COILS, 2 * LINES, 2 * N), F32),
+            pltpu.VMEM((2, EARLY, 2, N, N), BF16),
             pltpu.VMEM((4 * LINES, 2 * N), BF16),
             pltpu.VMEM((2 * N, 4 * LINES), BF16),
             jax.ShapeDtypeStruct((2 * GROUP * GROUP, 2 * RANK), BF16),
         ),
-        in_specs=[HBM] * 5,
-        out_specs=(VMEM,) * 4,
+        in_specs=[HBM] * 6,
+        out_specs=(VMEM,) * 5,
         scratch_shapes=[
             pltpu.VMEM((2, COILS, 2, LINES, N), F32),
             pltpu.VMEM((1, LINES), jnp.int32),
@@ -276,30 +282,33 @@
             pltpu.VMEM((2 * RANK, GROUP * GROUP), BF16),
             pltpu.VMEM((GROUP * GROUP, GROUP * GROUP), BF16),
             DMA((COILS // CHUNK,)),
-            DMA((4,)),
+            DMA((5,)),
         ],
         compiler_params=pltpu.CompilerParams(vmem_limit_bytes=16 * MIB),
         name="data_back",
-    )(*map(in_hbm, (data, lines, dft, temporal, order)))
+    )(*map(in_hbm, (data, coils, lines, dft, temporal, order)))
 
 
 def model_kernel(
-    images_ref, back_ref, ahead_ref, adjoint_ref, coils_hbm, depth_hbm, lane_hbm, panel_hbm,
-    out_ref, coils_ref, depth_ref, lane_ref, panel_ref, field_ref, grad_ref,
-    lines_ref, rows_ref, coil_sems, sems,
+    images_ref, back_ref, early_ref, ahead_ref, adjoint_ref, coils_hbm, depth_hbm, panel_hbm,
+    out_ref, coils_ref, depth_ref, panel_ref, field_ref, grad_ref,
+    lines_ref, rows_ref, resid_ref, coil_sems, sems,
 ):
     def coil_copy(coil, part):
         return pltpu.make_async_copy(
             coils_hbm.at[part, coil], coils_ref.at[part, coil], coil_sems.at[part, coil]
         )
 
-    for coil in range(COILS):
-        for part in range(2):
-            coil_copy(coil, part).start()
+    def coil_group(group):
+        return [coil_copy(coil, part) for coil in GROUPS[group] for part in range(2)]
+
+    for group in range(2):
+        for copy in coil_group(group):
+            copy.start()
     orders = [
         pltpu.make_async_copy(source, target, sems.at[i])
         for i, (source, target) in enumerate(
-            [(depth_hbm, depth_ref), (lane_hbm, lane_ref), (panel_hbm, panel_ref)]
+            [(depth_hbm, depth_ref), (panel_hbm, panel_ref)]
         )
     ]
     for copy in orders:
@@ -314,7 +323,6 @@
                 field_ref[part, here, block * 128 : (block + 1) * 128] = values[
                     block * PART : (block + 1) * PART
                 ]
-    grad_ref[...] = jnp.zeros_like(grad_ref)
     lines_ref[:, 0 : 2 * N] = ahead_ref[...]
     lines_ref[0:96, 2 * N : 4 * N] = ahead_ref[0:96, :]
     lines_ref[96:192, 2 * N : 4 * N] = jnp.zeros((96, 2 * N), BF16)
@@ -322,78 +330,99 @@
     rows_ref[:, 96:192] = adjoint_ref[:, 0:96]
     rows_ref[:, 192:288] = adjoint_ref[:, 96:192]
 
-    def one_coil(coil):
-        coil_re, coil_im = (
-            jnp.concatenate([coils_ref[part, coil, 0], coils_ref[part, coil, 1]], 1).astype(F32)
+    def coil_pair(coil, source):
+        return (
+            jnp.concatenate([source[part, coil, 0], source[part, coil, 1]], 1).astype(F32)
             for part in range(2)
         )
+
+    def ahead_one(coil, source):
+        coil_re, coil_im = coil_pair(coil, source)
         field_re, field_im = field_ref[0], field_ref[1]
         re_high, re_low = split(coil_re * field_re - coil_im * field_im)
         im_high, im_low = split(coil_re * field_im + coil_im * field_re)
         first = dot(lines_ref[...], jnp.concatenate([re_high, im_high, re_low, im_low], 0))
         high, low = split(first[0:96] + first[96:192] - back_ref[coil])
-        rows = dot(rows_ref[...], jnp.concatenate([high, low, high], 0))
+        resid_ref[coil, 0:96] = high
+        resid_ref[coil, 96:192] = low
+        resid_ref[coil, 192:288] = high
+
+    def back_one(coil, source):
+        coil_re, coil_im = coil_pair(coil, source)
+        rows = dot(rows_ref[...], resid_ref[coil])
         rows_re, rows_im = rows[0:N], rows[N : 2 * N]
-        grad_ref[0] += coil_re * rows_re + coil_im * rows_im
-        grad_ref[1] += coil_re * rows_im - coil_im * rows_re
-
-    def some_coils(step, carry):
-        for i in range(CHUNK):
-            for part in range(2):
-                coil_copy(step * CHUNK + i, part).wait()
-        for i in range(CHUNK):
-            one_coil(step * CHUNK + i)
+        return coil_re * rows_re + coil_im * rows_im, coil_re * rows_im - coil_im * rows_re
+
+    for coil in range(EARLY):
+        ahead_one(coil, early_ref)
+    for group, coils in enumerate(GROUPS):
+        for copy in coil_group(group):
+            copy.wait()
+        if group + 2 < len(GROUPS):
+            for copy in coil_group(group + 2):
+                copy.start()
+        for coil in coils:
+            ahead_one(coil, coils_ref)
+    for coil in range(EARLY):
+        grad_ref[0], grad_ref[1] = back_one(coil, early_ref)
+
+    def some_back(step, carry):
+        for i in range(TOGETHER):
+            grad_re, grad_im = back_one(EARLY + step * TOGETHER + i, coils_ref)
+            grad_ref[0] += grad_re
+            grad_ref[1] += grad_im
         return carry
 
-    lax.fori_loop(0, COILS // CHUNK, some_coils, 0)
+    lax.fori_loop(0, (COILS - EARLY) // TOGETHER, some_back, 0)
     for copy in orders:
         copy.wait()
-    total = jnp.zeros((N, 4 * N), F32)
-    for channel in range(4):
-        order = lane_ref[channel * N : (channel + 1) * N, :]
-        for term in split(grad_ref[channel // 2, :, channel % 2 * N : (channel % 2 + 1) * N]):
-            total = total + dot(dot(depth_ref[...], term, (1, 1)).astype(BF16), order)
-    real = total[:, 0:WIDE].reshape(PART, GROUP, WIDE)
-    imag = total[:, WIDE : 2 * WIDE].reshape(PART, GROUP, WIDE)
-    largest = jnp.max(jnp.maximum(jnp.abs(real), jnp.abs(imag)), axis=0)
-    largest = jnp.max(largest.T.reshape(GROUP, 2 * PART, GROUP), axis=1)
-    level = level_of(largest).T
-    high, low = split(level)
+    parts = []
+    for part in range(2):
+        for pos in range(2):
+            high, low = split(grad_ref[part, :, pos * N : (pos + 1) * N])
+            moved = dot(depth_ref[...], high, (1, 1)) + dot(depth_ref[...], low, (1, 1))
+            parts.append(moved.reshape(PART, GROUP, N))
+    largest = functools.reduce(jnp.maximum, map(jnp.abs, parts))
+    largest = jnp.max(largest, axis=0)
+    for shift in (1, 2, 4, 4):
+        ahead = jnp.concatenate([largest[:, shift:], largest[:, :shift]], 1)
+        largest = jnp.maximum(largest, ahead)
+    high, low = split(level_of(largest))
     level = dot(high, panel_ref[...]) + dot(low, panel_ref[...])
     scale = scale_down(level)[None]
-    words = pair_up(real * scale, imag * scale)
+    words = [pair_up(parts[pos] * scale, parts[2 + pos] * scale) for pos in range(2)]
     level = level.astype(jnp.int32)
     for d in range(GROUP):
-        lanes = slice(d * 2 * PART, (d + 1) * 2 * PART)
-        pieces = [words[zz, :, lanes] for zz in range(PART)]
-        pieces += [level[:, lanes]] * (WIDE // (2 * PART) - PART)
+        lanes = slice(d * PART, (d + 1) * PART)
+        pieces = [words[pos][zz, :, lanes] for zz in range(PART) for pos in range(2)]
+        pieces.append(jnp.broadcast_to(level[:, d * PART : d * PART + 1], (GROUP, WIDE - VOX)))
         out_ref[d * GROUP : (d + 1) * GROUP, 0, :] = jnp.concatenate(pieces, 1)
 
 
-def model(images, back, ahead, adjoint, coils, depth_order, lane_order, panel):
+def model(images, back, early, ahead, adjoint, coils, depth_order, panel):
     return pl.pallas_call(
         model_kernel,
         out_shape=jax.ShapeDtypeStruct((GROUP * GROUP, 1, WIDE), jnp.int32),
-        in_specs=[VMEM] * 4 + [HBM] * 4,
+        in_specs=[VMEM] * 5 + [HBM] * 3,
         out_specs=VMEM,
         scratch_shapes=[
             pltpu.VMEM((2, COILS, 2, N, N), BF16),
             pltpu.VMEM((N, N), BF16),
-            pltpu.VMEM((4 * N, 4 * N), BF16),
-            pltpu.VMEM((GROUP, WIDE), BF16),
+            pltpu.VMEM((N, N), BF16),
             pltpu.VMEM((2, N, 2 * N), F32),
             pltpu.VMEM((2, N, 2 * N), F32),
             pltpu.VMEM((4 * LINES, 4 * N), BF16),
             pltpu.VMEM((2 * N, 6 * LINES), BF16),
+            pltpu.VMEM((COILS, 6 * LINES, 2 * N), BF16),
             DMA((2, COILS)),
-            DMA((3,)),
+            DMA((2,)),
         ],
-        compiler_params=pltpu.CompilerParams(vmem_limit_bytes=24 * MIB),
+        compiler_params=pltpu.CompilerParams(vmem_limit_bytes=32 * MIB),
         name="model",
     )(
         images,
-        *map(in_vmem, (back, ahead, adjoint)),
-        *map(in_hbm, (coils, depth_order, lane_order, panel)),
+        *map(in_vmem, (back, early, ahead, adjoint)),
+        *map(in_hbm, (coils, depth_order, panel)),
     )
 
 
@@ -423,15 +452,14 @@
 def on_device(spatial_basis, temporal, coil_maps, kspace_data, sampled_lines):
     table = {name: jnp.asarray(value) for name, value in constants().items()}
     flat_temporal = temporal.reshape(2 * RANK, GROUP * GROUP)
-    flat_basis = jnp.transpose(spatial_basis, (0, 1, 3, 2, 4)).reshape(-1, N)
+    flat_basis = jnp.transpose(spatial_basis, (0, 1, 3, 2, 4)).reshape(-1, 2, N)
     sent = frames(flat_basis, flat_temporal, table["spread"], table["inside"])
     images = lax.all_to_all(sent, "dev", 0, 0, tiled=True)
-    back, ahead, adjoint, weights = data_back(
-        kspace_data, sampled_lines, table["dft"], flat_temporal, table["frame_order"]
+    back, early, ahead, adjoint, weights = data_back(
+        kspace_data, coil_maps, sampled_lines, table["dft"], flat_temporal, table["frame_order"]
     )
     sent = model(
-        images, back, ahead, adjoint, coil_maps,
-        table["depth_order"], table["lane_order"], table["panel"],
+        images, back, early, ahead, adjoint, coil_maps, table["depth_order"], table["panel"]
     )
     grads = lax.all_to_all(sent, ("dev", "grp"), 0, 0, tiled=True)
     slab = lax.dynamic_slice_in_dim(spatial_basis, lax.axis_index("grp") * PART, PART, 4)

time: 68.1 us -> 63.8 us (0.937)
  local copies, waits for them, and re-layouts: 2.78 us -> 0.52 us
  Pallas kernels: 25.2 us -> 23.1 us
    pallas_call x1, Pallas kernels: 15.1 us -> 12.7 us  [model(): pl.pallas_call(model_kernel, out_shape=jax.ShapeDtypeStruct((GROUP * GROU...]
    reshape x1 -> x0, local copies, waits for them, and re-layouts: 2.26 us -> none  [on_device(): flat_basis = jnp.transpose(spatial_basis, (0, 1, 3, 2, 4)).reshape(-1, N)]
where the time goes in v3:
time: 63.8 us; the launch traced here: 63.5 us
  Pallas kernels  23.1 us (36%)
  starting transfers between devices  19.6 us (31%)
  waiting for transfers between devices  18.6 us (29%)
  other arithmetic  1.65 us (3%)
    all_to_all x1, waiting for transfers between devices, on_device(): grads = lax.all_to_all(sent, ('dev', 'grp'), 0, 0, tiled=True)  16.2 us
    all_to_all x1, starting transfers between devices, on_device(): grads = lax.all_to_all(sent, ('dev', 'grp'), 0, 0, tiled=True)  12.7 us
    pallas_call x1, Pallas kernels, model(): pl.pallas_call(model_kernel, out_shape=jax.ShapeDtypeStruct((GROUP * GROU...  12.7 us
    all_to_all x1, starting transfers between devices, on_device(): images = lax.all_to_all(sent, 'dev', 0, 0, tiled=True)  6.84 us
    pallas_call x1, Pallas kernels, data_back(): pl.pallas_call(data_kernel, out_shape=(pltpu.VMEM((COILS, 2 * LINES, 2 *...  5.28 us
    pallas_call x1, Pallas kernels, frames(): pl.pallas_call(frames_kernel, out_shape=jax.ShapeDtypeStruct((GROUP, 40,...  3.43 us
    all_to_all x1, waiting for transfers between devices, on_device(): images = lax.all_to_all(sent, 'dev', 0, 0, tiled=True)  2.33 us
    pallas_call x1, Pallas kernels, update(): pl.pallas_call(update_kernel, out_shape=jax.ShapeDtypeStruct((2, 2 * PART...  1.68 us
  transfers between devices with their start and end apart: 2, of which 2 were waited for; matrix products, arithmetic and copies ran while one was open for 3% of the time, Pallas kernels for 8%

profile of v3, /device:TPU:1, one launch (start us, length us, event | category | flops | bytes accessed | tf_op | source)
XLA Modules:
  0.0 63.5 jit_solution(15553231097269771785)
XLA Ops:
  0.0 3.4 %frames.1 = s32[16,40,128]{2,1,0:T(8,128)} custom-call(bf16[768,2,192]{2,1,0:T(2,128)(2,1)} %bitcast.11, bf16[64,256]{1,0:T(8,128)(2,1)} %bitcast.12, bf16[64,1536]{1,0:T(8,128)(2,1)} %constant.26.clone.spread_hbm, f32[24,1536]{1,0:T(8,128)} %constant.27.clone.inside_hbm), custom_call_target="tpu_custom_call" | custom-call | tf_op jit(solution)/shard_map/frames/pallas_call | solution.py:167
  3.4 6.8 %all-to-all-start = ((s32[16,40,128]{2,1,0:T(8,128)}), s32[16,40,128]{2,1,0:T(8,128)S(1)}, u32[]{:S(2)}, u32[]{:S(2)}) async-start(s32[16,40,128]{2,1,0:T(8,128)} %frames.1), calls=%async_computation | async-start | bytes 655360 | tf_op jit(solution)/shard_map/all_to_all | solution.py:457
  10.3 5.3 %data_back.1 = (f32[16,96,384]{2,1,0:T(8,128)S(1)}, bf16[2,1,2,192,192]{4,3,2,1,0:T(8,128)(2,1)S(1)}, bf16[192,384]{1,0:T(8,128)(2,1)S(1)}, bf16[384,192]{1,0:T(8,128)(2,1)S(1)}, bf16[512,64]{1,0:T(8,128)(2,1)S(1)}) custom-call(f32[1,2,16,2,48,192]{5,4,3,2,1,0:T(8,128)} %data_hbm.1, bf16[2,16,2,192,192]{4,3,2,1,0:T(8,128)(2,1)} %coils_hbm.3, ...), custom_call_target="tpu_custom_call" | custom-call | tf_op jit(solution)/shard_map/data_back/pallas_call | solution.py:267
  15.6 2.3 %all-to-all-done.images_ref = s32[16,40,128]{2,1,0:T(8,128)S(1)} async-done(((s32[16,40,128]{2,1,0:T(8,128)}), s32[16,40,128]{2,1,0:T(8,128)S(1)}, u32[]{:S(2)}, u32[]{:S(2)}) %all-to-all-start) | async-done | bytes 327712 | tf_op jit(solution)/shard_map/all_to_all | solution.py:457
  17.9 12.7 %model.1 = s32[256,1,384]{2,1,0:T(1,128)} custom-call(s32[16,40,128]{2,1,0:T(8,128)S(1)} %all-to-all-done.images_ref, f32[16,96,384]{2,1,0:T(8,128)S(1)} %get-tuple-element.10.back_ref, bf16[2,1,2,192,192]{4,3,2,1,0:T(8,128)(2,1)S(1)} %get-tuple-element.11.early_ref, bf16[192,384]{1,0:T(8,128)(2,1)S(1)} %get-tuple-element.12.ahead_ref, ...), custom_call_target="tpu_custom_call" | custom-call | tf_op jit(solution)/shard_map/model/pallas_call | solution.py:403
  30.6 0.0 copy-start
  30.6 12.7 %all-to-all-start.1 = ((s32[256,1,384]{2,1,0:T(1,128)}), s32[256,1,384]{2,1,0:T(1,128)S(1)}, u32[]{:S(2)}, u32[]{:S(2)}) async-start(s32[256,1,384]{2,1,0:T(1,128)} %model.1), calls=%async_computation.1 | async-start | bytes 786432 | tf_op jit(solution)/shard_map/all_to_all | solution.py:464
  43.4 1.6 %convert_bitcast_fusion = f32[2,12,12,2,32]{2,3,1,4,0:T(2,128)S(1)} fusion(bf16[2,32,2,12,192]{4,2,3,1,0:T(2,128)(2,1)} %param.12, s32[]{:T(128)S(6)} %select_n.3), kind=kLoop, calls=%fused_computation | loop fusion | flops 18432 | bytes 110596 | tf_op jit(solution)/shard_map/convert_element_type | solution.py:466
  45.0 0.5 copy.13
  45.6 16.2 %all-to-all-done.1.grads_ref = s32[256,1,384]{2,1,0:T(1,128)S(1)} async-done(((s32[256,1,384]{2,1,0:T(1,128)}), s32[256,1,384]{2,1,0:T(1,128)S(1)}, u32[]{:S(2)}, u32[]{:S(2)}) %all-to-all-start.1) | async-done | bytes 393248 | tf_op jit(solution)/shard_map/all_to_all | solution.py:464
  61.8 0.0 copy-done
  61.8 1.7 %update.1 = f32[2,288,32]{2,1,0:T(8,128)} custom-call(s32[256,1,384]{2,1,0:T(1,128)S(1)} %all-to-all-done.1.grads_ref, bf16[512,64]{1,0:T(8,128)(2,1)S(1)} %get-tuple-element.14.weights_ref, bf16[288,288]{1,0:T(8,128)(2,1)S(1)} %copy-done, f32[2,288,32]{2,1,0:T(8,128)S(1)} %bitcast.10), custom_call_target="tpu_custom_call" | custom-call | tf_op jit(solution)/shard_map/update/pallas_call | solution.py:442
Async XLA Ops:
  3.4 14.5 %all-to-all-start = ((s32[16,40,128]{2,1,0:T(8,128)}), s32[16,40,128]{2,1,0:T(8,128)S(1)}, u32[]{:S(2)}, u32[]{:S(2)}) async-start(s32[16,40,128]{2,1,0:T(8,128)} %frames.1), calls=%async_computation | async-start | bytes 655360 | tf_op jit(solution)/shard_map/all_to_all | solution.py:457
  30.6 31.2 %copy-start = (bf16[288,288]{1,0:T(8,128)(2,1)S(1)}, bf16[288,288]{1,0:T(8,128)(2,1)}, u32[]{:S(2)}) copy-start(bf16[288,288]{1,0:T(8,128)(2,1)} %constant.30.clone.pick_ref) | copy-start | bytes 497668
  30.6 31.2 %all-to-all-start.1 = ((s32[256,1,384]{2,1,0:T(1,128)}), s32[256,1,384]{2,1,0:T(1,128)S(1)}, u32[]{:S(2)}, u32[]{:S(2)}) async-start(s32[256,1,384]{2,1,0:T(1,128)} %model.1), calls=%async_computation.1 | async-start | bytes 786432 | tf_op jit(solution)/shard_map/all_to_all | solution.py:464

commit v4 on v3

--- a/solution.py
+++ b/solution.py
@@ -12,13 +12,13 @@
 STEP_SIZE = 0.25
 N = 192
 PART = 12
+ROWS = 4
 RANK = 32
 COILS = 16
 LINES = 48
 EARLY = 1
-GROUPS = [range(1, 3), range(3, 6), range(6, 11), range(11, 16)]
+GROUPS = [[(0,)], [(1, 2)], [(3, 4), (5, 6)], [(7, 8), (9, 10)], [(11, 12), (13, 14), (15,)]]
 CHUNK = 4
-TOGETHER = 15
 GROUP = 16
 VOX = 2 * PART * PART
 WIDE = 384
@@ -83,10 +83,10 @@
     cos_pair = two_terms(np.cos(angles) / math.sqrt(N))
     sin_pair = two_terms(np.sin(angles) / math.sqrt(N))
     dft = np.stack([*cos_pair, *sin_pair])
-    columns = np.arange(2 * RANK * 2 * PART)
-    spread = (columns[None, :] // (2 * PART) == np.arange(2 * RANK)[:, None])
-    rows = np.arange(2 * PART)
-    inside = (columns[None, :] % (2 * PART) == ((rows % PART) * 2 + rows // PART)[:, None])
+    columns = np.arange(2 * RANK * 2 * ROWS)
+    spread = columns[None, :] // (2 * ROWS) == np.arange(2 * RANK)[:, None]
+    rows = np.arange(2 * ROWS)
+    inside = columns[None, :] % (2 * ROWS) == ((rows % ROWS) * 2 + rows // ROWS)[:, None]
     order = np.arange(N)
     depth_order = ((order % GROUP) * PART + order // GROUP)[:, None] == places[None, :]
     peers = np.arange(GROUP * GROUP)
@@ -108,7 +108,7 @@
 
 def frames_kernel(
     basis_hbm, temporal_hbm, spread_hbm, inside_hbm, out_ref,
-    basis_ref, temporal_ref, spread_ref, inside_ref, mix_ref, sems,
+    basis_ref, temporal_ref, spread_ref, inside_ref, mix_ref, basis_sem, sems,
 ):
     copies = [
         pltpu.make_async_copy(source, target, sems.at[i])
@@ -117,10 +117,11 @@
                 (temporal_hbm, temporal_ref),
                 (spread_hbm, spread_ref),
                 (inside_hbm, inside_ref),
-                (basis_hbm, basis_ref),
             ]
         )
     ]
+    whole = pltpu.make_async_copy(basis_hbm, basis_ref, basis_sem)
+    whole.start()
     for copy in copies:
         copy.start()
     copies[0].wait()
@@ -140,42 +141,42 @@
     wide_im = dot(swapped.astype(BF16), spread_ref[...])
     copies[2].wait()
     inside = inside_ref[...]
-    for f in range(GROUP):
-        block = jnp.concatenate(
-            [inside * wide_re[f : f + 1], inside * wide_im[f : f + 1]], axis=0
-        )
-        mix_ref[f * 48 : (f + 1) * 48, :] = block.astype(BF16)
-    copies[3].wait()
-    basis = basis_ref[...].reshape(2 * RANK * 2 * PART, N)
-    images = dot(mix_ref[...], basis)
-    for f in range(GROUP):
-        image = images[f * 48 : (f + 1) * 48]
-        largest = jnp.max(jnp.max(jnp.abs(image), axis=0, keepdims=True), axis=1, keepdims=True)
-        level = level_of(largest)
-        image = image * scale_down(level)
-        words = pair_up(image[0:24], image[24:48])
-        words = jnp.concatenate([words[0:PART], words[PART : 2 * PART]], 1)
+    wide = jnp.concatenate([wide_re[:, None], wide_im[:, None]], 1)
+    mix = inside[None, None] * wide[:, :, None]
+    mix_ref[...] = mix.reshape(2 * GROUP * 2 * ROWS, wide_re.shape[1]).astype(BF16)
+    images = []
+    whole.wait()
+    for i in range(PART // ROWS):
+        basis = basis_ref[:, i * ROWS : (i + 1) * ROWS].reshape(2 * RANK * 2 * ROWS, N)
+        images.append(dot(mix_ref[...], basis).reshape(GROUP, 2, 2 * ROWS, N))
+    largest = functools.reduce(jnp.maximum, [jnp.max(jnp.abs(image), axis=1) for image in images])
+    largest = jnp.max(jnp.max(largest, axis=1, keepdims=True), axis=2, keepdims=True)
+    level = level_of(largest)
+    scale = scale_down(level)
+    for i, image in enumerate(images):
+        words = pair_up(image[:, 0] * scale, image[:, 1] * scale)
+        words = jnp.concatenate([words[:, 0:ROWS], words[:, ROWS : 2 * ROWS]], 2)
         for block in range(3):
-            out_ref[f, block * PART : (block + 1) * PART, :] = words[
-                :, block * 128 : (block + 1) * 128
-            ]
-        out_ref[f, 36:40, :] = jnp.broadcast_to(level, (4, 128)).astype(jnp.int32)
+            at = block * PART + i * ROWS
+            out_ref[:, at : at + ROWS, :] = words[:, :, block * 128 : (block + 1) * 128]
+    out_ref[:, 36:40, :] = jnp.broadcast_to(level, (GROUP, 4, 128)).astype(jnp.int32)
 
 
 def frames(basis, temporal, spread, inside):
-    rows = 2 * RANK * 2 * PART
+    rows = 2 * RANK * 2 * ROWS
     return pl.pallas_call(
         frames_kernel,
         out_shape=jax.ShapeDtypeStruct((GROUP, 40, 128), jnp.int32),
         in_specs=[HBM] * 4,
         out_specs=VMEM,
         scratch_shapes=[
-            pltpu.VMEM((rows // 2, 2, N), BF16),
+            pltpu.VMEM((2 * RANK, PART, 2, N), BF16),
             pltpu.VMEM((2 * RANK, GROUP * GROUP), BF16),
             pltpu.VMEM((2 * RANK, rows), BF16),
-            pltpu.VMEM((2 * PART, rows), F32),
-            pltpu.VMEM((GROUP * 48, rows), BF16),
-            DMA((4,)),
+            pltpu.VMEM((2 * ROWS, rows), F32),
+            pltpu.VMEM((2 * GROUP * 2 * ROWS, rows), BF16),
+            DMA(()),
+            DMA((3,)),
         ],
         compiler_params=pltpu.CompilerParams(vmem_limit_bytes=16 * MIB),
         name="frames",
@@ -300,7 +301,8 @@
         )
 
     def coil_group(group):
-        return [coil_copy(coil, part) for coil in GROUPS[group] for part in range(2)]
+        coils = [coil for pair in GROUPS[group] for coil in pair if coil >= EARLY]
+        return [coil_copy(coil, part) for coil in coils for part in range(2)]
 
     for group in range(2):
         for copy in coil_group(group):
@@ -330,50 +332,58 @@
     rows_ref[:, 96:192] = adjoint_ref[:, 0:96]
     rows_ref[:, 192:288] = adjoint_ref[:, 96:192]
 
-    def coil_pair(coil, source):
+    def coil_maps(coil):
+        source = early_ref if coil < EARLY else coils_ref
         return (
             jnp.concatenate([source[part, coil, 0], source[part, coil, 1]], 1).astype(F32)
             for part in range(2)
         )
 
-    def ahead_one(coil, source):
-        coil_re, coil_im = coil_pair(coil, source)
+    def terms_of(coil):
+        coil_re, coil_im = coil_maps(coil)
         field_re, field_im = field_ref[0], field_ref[1]
         re_high, re_low = split(coil_re * field_re - coil_im * field_im)
         im_high, im_low = split(coil_re * field_im + coil_im * field_re)
-        first = dot(lines_ref[...], jnp.concatenate([re_high, im_high, re_low, im_low], 0))
-        high, low = split(first[0:96] + first[96:192] - back_ref[coil])
-        resid_ref[coil, 0:96] = high
-        resid_ref[coil, 96:192] = low
-        resid_ref[coil, 192:288] = high
-
-    def back_one(coil, source):
-        coil_re, coil_im = coil_pair(coil, source)
-        rows = dot(rows_ref[...], resid_ref[coil])
-        rows_re, rows_im = rows[0:N], rows[N : 2 * N]
-        return coil_re * rows_re + coil_im * rows_im, coil_re * rows_im - coil_im * rows_re
-
-    for coil in range(EARLY):
-        ahead_one(coil, early_ref)
-    for group, coils in enumerate(GROUPS):
+        return jnp.concatenate([re_high, im_high, re_low, im_low], 0)
+
+    def side(values, i):
+        return values[:, i * 2 * N : (i + 1) * 2 * N]
+
+    def go_ahead(coils):
+        first = dot(lines_ref[...], jnp.concatenate([terms_of(coil) for coil in coils], 1))
+        for i, coil in enumerate(coils):
+            here = side(first, i)
+            high, low = split(here[0:96] + here[96:192] - back_ref[coil])
+            resid_ref[coil, 0:96] = high
+            resid_ref[coil, 96:192] = low
+            resid_ref[coil, 192:288] = high
+
+    def go_back(coils):
+        both = dot(rows_ref[...], jnp.concatenate([resid_ref[coil] for coil in coils], 1))
+        total_re = total_im = 0.0
+        for i, coil in enumerate(coils):
+            coil_re, coil_im = coil_maps(coil)
+            rows_re, rows_im = side(both, i)[0:N], side(both, i)[N : 2 * N]
+            total_re += coil_re * rows_re + coil_im * rows_im
+            total_im += coil_re * rows_im - coil_im * rows_re
+        return total_re, total_im
+
+    for group, pairs in enumerate(GROUPS):
         for copy in coil_group(group):
             copy.wait()
         if group + 2 < len(GROUPS):
             for copy in coil_group(group + 2):
                 copy.start()
-        for coil in coils:
-            ahead_one(coil, coils_ref)
-    for coil in range(EARLY):
-        grad_ref[0], grad_ref[1] = back_one(coil, early_ref)
-
-    def some_back(step, carry):
-        for i in range(TOGETHER):
-            grad_re, grad_im = back_one(EARLY + step * TOGETHER + i, coils_ref)
-            grad_ref[0] += grad_re
-            grad_ref[1] += grad_im
-        return carry
-
-    lax.fori_loop(0, (COILS - EARLY) // TOGETHER, some_back, 0)
+        for coils in pairs:
+            go_ahead(coils)
+    for group, pairs in enumerate(GROUPS):
+        for i, coils in enumerate(pairs):
+            grad_re, grad_im = go_back(coils)
+            if group == i == 0:
+                grad_ref[0], grad_ref[1] = grad_re, grad_im
+            else:
+                grad_ref[0] += grad_re
+                grad_ref[1] += grad_im
     for copy in orders:
         copy.wait()
     parts = []
@@ -452,7 +462,7 @@
 def on_device(spatial_basis, temporal, coil_maps, kspace_data, sampled_lines):
     table = {name: jnp.asarray(value) for name, value in constants().items()}
     flat_temporal = temporal.reshape(2 * RANK, GROUP * GROUP)
-    flat_basis = jnp.transpose(spatial_basis, (0, 1, 3, 2, 4)).reshape(-1, 2, N)
+    flat_basis = jnp.transpose(spatial_basis, (0, 1, 3, 2, 4)).reshape(2 * RANK, PART, 2, N)
     sent = frames(flat_basis, flat_temporal, table["spread"], table["inside"])
     images = lax.all_to_all(sent, "dev", 0, 0, tiled=True)
     back, early, ahead, adjoint, weights = data_back(

time: 63.8 us -> 62.4 us (0.978)
  Pallas kernels: 23.1 us -> 21.6 us
    pallas_call x1, Pallas kernels: 12.7 us -> 11.8 us  [model(): pl.pallas_call(model_kernel, out_shape=jax.ShapeDtypeStruct((GROUP * GROU...]
  transfers between devices with their start and end apart: 2 -> 2, of which waited for: 2 -> 2; matrix products, arithmetic and copies ran while one was open for 3% -> 3% of each run, Pallas kernels for 8% -> 9%
where the time goes in v4:
time: 62.4 us; the launch traced here: 62.1 us
  Pallas kernels  21.6 us (35%)
  starting transfers between devices  19.8 us (32%)
  waiting for transfers between devices  18.6 us (30%)
  other arithmetic  1.65 us (3%)
    all_to_all x1, waiting for transfers between devices, on_device(): grads = lax.all_to_all(sent, ('dev', 'grp'), 0, 0, tiled=True)  16.2 us
    all_to_all x1, starting transfers between devices, on_device(): grads = lax.all_to_all(sent, ('dev', 'grp'), 0, 0, tiled=True)  12.9 us
    pallas_call x1, Pallas kernels, model(): pl.pallas_call(model_kernel, out_shape=jax.ShapeDtypeStruct((GROUP * GROU...  11.8 us
    all_to_all x1, starting transfers between devices, on_device(): images = lax.all_to_all(sent, 'dev', 0, 0, tiled=True)  6.84 us
    pallas_call x1, Pallas kernels, data_back(): pl.pallas_call(data_kernel, out_shape=(pltpu.VMEM((COILS, 2 * LINES, 2 *...  5.28 us
    pallas_call x1, Pallas kernels, frames(): pl.pallas_call(frames_kernel, out_shape=jax.ShapeDtypeStruct((GROUP, 40,...  2.81 us
    all_to_all x1, waiting for transfers between devices, on_device(): images = lax.all_to_all(sent, 'dev', 0, 0, tiled=True)  2.33 us
    pallas_call x1, Pallas kernels, update(): pl.pallas_call(update_kernel, out_shape=jax.ShapeDtypeStruct((2, 2 * PART...  1.68 us
  transfers between devices with their start and end apart: 2, of which 2 were waited for; matrix products, arithmetic and copies ran while one was open for 3% of the time, Pallas kernels for 9%

profile of v4, /device:TPU:1, one launch (start us, length us, event | category | flops | bytes accessed | tf_op | source)
XLA Modules:
  0.0 62.1 jit_solution(9960374855554093332)
XLA Ops:
  0.0 2.8 %frames.1 = s32[16,40,128]{2,1,0:T(8,128)} custom-call(bf16[64,12,2,192]{3,2,1,0:T(2,128)(2,1)} %bitcast.11, bf16[64,256]{1,0:T(8,128)(2,1)} %bitcast.12, bf16[64,512]{1,0:T(8,128)(2,1)} %constant.26.clone.spread_hbm, f32[8,512]{1,0:T(8,128)} %constant.27.clone.inside_hbm), custom_call_target="tpu_custom_call" | custom-call | tf_op jit(solution)/shard_map/frames/pallas_call | solution.py:167
  2.8 6.8 %all-to-all-start = ((s32[16,40,128]{2,1,0:T(8,128)}), s32[16,40,128]{2,1,0:T(8,128)S(1)}, u32[]{:S(2)}, u32[]{:S(2)}) async-start(s32[16,40,128]{2,1,0:T(8,128)} %frames.1), calls=%async_computation | async-start | bytes 655360 | tf_op jit(solution)/shard_map/all_to_all | solution.py:467
  9.7 5.3 %data_back.1 = (f32[16,96,384]{2,1,0:T(8,128)S(1)}, bf16[2,1,2,192,192]{4,3,2,1,0:T(8,128)(2,1)S(1)}, bf16[192,384]{1,0:T(8,128)(2,1)S(1)}, bf16[384,192]{1,0:T(8,128)(2,1)S(1)}, bf16[512,64]{1,0:T(8,128)(2,1)S(1)}) custom-call(f32[1,2,16,2,48,192]{5,4,3,2,1,0:T(8,128)} %data_hbm.1, bf16[2,16,2,192,192]{4,3,2,1,0:T(8,128)(2,1)} %coils_hbm.3, ...), custom_call_target="tpu_custom_call" | custom-call | tf_op jit(solution)/shard_map/data_back/pallas_call | solution.py:268
  14.9 2.3 %all-to-all-done.images_ref = s32[16,40,128]{2,1,0:T(8,128)S(1)} async-done(((s32[16,40,128]{2,1,0:T(8,128)}), s32[16,40,128]{2,1,0:T(8,128)S(1)}, u32[]{:S(2)}, u32[]{:S(2)}) %all-to-all-start) | async-done | bytes 327712 | tf_op jit(solution)/shard_map/all_to_all | solution.py:467
  17.3 11.8 %model.1 = s32[256,1,384]{2,1,0:T(1,128)} custom-call(s32[16,40,128]{2,1,0:T(8,128)S(1)} %all-to-all-done.images_ref, f32[16,96,384]{2,1,0:T(8,128)S(1)} %get-tuple-element.10.back_ref, bf16[2,1,2,192,192]{4,3,2,1,0:T(8,128)(2,1)S(1)} %get-tuple-element.11.early_ref, bf16[192,384]{1,0:T(8,128)(2,1)S(1)} %get-tuple-element.12.ahead_ref, ...), custom_call_target="tpu_custom_call" | custom-call | tf_op jit(solution)/shard_map/model/pallas_call | solution.py:413
  29.1 0.0 copy-start
  29.1 12.9 %all-to-all-start.1 = ((s32[256,1,384]{2,1,0:T(1,128)}), s32[256,1,384]{2,1,0:T(1,128)S(1)}, u32[]{:S(2)}, u32[]{:S(2)}) async-start(s32[256,1,384]{2,1,0:T(1,128)} %model.1), calls=%async_computation.1 | async-start | bytes 786432 | tf_op jit(solution)/shard_map/all_to_all | solution.py:474
  42.0 1.6 %convert_bitcast_fusion = f32[2,12,12,2,32]{2,3,1,4,0:T(2,128)S(1)} fusion(bf16[2,32,2,12,192]{4,2,3,1,0:T(2,128)(2,1)} %param.12, s32[]{:T(128)S(6)} %select_n.3), kind=kLoop, calls=%fused_computation | loop fusion | flops 18432 | bytes 110596 | tf_op jit(solution)/shard_map/convert_element_type | solution.py:476
  43.7 0.5 copy.13
  44.2 16.2 %all-to-all-done.1.grads_ref = s32[256,1,384]{2,1,0:T(1,128)S(1)} async-done(((s32[256,1,384]{2,1,0:T(1,128)}), s32[256,1,384]{2,1,0:T(1,128)S(1)}, u32[]{:S(2)}, u32[]{:S(2)}) %all-to-all-start.1) | async-done | bytes 393248 | tf_op jit(solution)/shard_map/all_to_all | solution.py:474
  60.4 0.0 copy-done
  60.4 1.7 %update.1 = f32[2,288,32]{2,1,0:T(8,128)} custom-call(s32[256,1,384]{2,1,0:T(1,128)S(1)} %all-to-all-done.1.grads_ref, bf16[512,64]{1,0:T(8,128)(2,1)S(1)} %get-tuple-element.14.weights_ref, bf16[288,288]{1,0:T(8,128)(2,1)S(1)} %copy-done, f32[2,288,32]{2,1,0:T(8,128)S(1)} %bitcast.10), custom_call_target="tpu_custom_call" | custom-call | tf_op jit(solution)/shard_map/update/pallas_call | solution.py:452
Async XLA Ops:
  2.8 14.5 %all-to-all-start = ((s32[16,40,128]{2,1,0:T(8,128)}), s32[16,40,128]{2,1,0:T(8,128)S(1)}, u32[]{:S(2)}, u32[]{:S(2)}) async-start(s32[16,40,128]{2,1,0:T(8,128)} %frames.1), calls=%async_computation | async-start | bytes 655360 | tf_op jit(solution)/shard_map/all_to_all | solution.py:467
  29.1 31.4 %copy-start = (bf16[288,288]{1,0:T(8,128)(2,1)S(1)}, bf16[288,288]{1,0:T(8,128)(2,1)}, u32[]{:S(2)}) copy-start(bf16[288,288]{1,0:T(8,128)(2,1)} %constant.30.clone.pick_ref) | copy-start | bytes 497668
  29.1 31.3 %all-to-all-start.1 = ((s32[256,1,384]{2,1,0:T(1,128)}), s32[256,1,384]{2,1,0:T(1,128)S(1)}, u32[]{:S(2)}, u32[]{:S(2)}) async-start(s32[256,1,384]{2,1,0:T(1,128)} %model.1), calls=%async_computation.1 | async-start | bytes 786432 | tf_op jit(solution)/shard_map/all_to_all | solution.py:474

commit v5 on v4

--- a/solution.py
+++ b/solution.py
@@ -21,6 +21,8 @@
 CHUNK = 4
 GROUP = 16
 VOX = 2 * PART * PART
+SLOT = 16
+LANES = 128
 WIDE = 384
 STEPS = 8.0
 TOP = 15.0
@@ -32,6 +34,33 @@
 in_vmem = lambda array: pltpu.with_memory_space_constraint(array, pltpu.VMEM)
 DMA = pltpu.SemaphoreType.DMA
 MIB = 1024 * 1024
+
+
+def swap_slots(pieces):
+    slot = lax.broadcasted_iota(jnp.int32, pieces[0].shape, 1) // SLOT
+    pieces = list(pieces)
+    for step in (1, 2, 4):
+        lower = jnp.bitwise_and(slot, step) == 0
+        for i in range(len(pieces)):
+            if i & step == 0:
+                first, second = pieces[i], pieces[i + step]
+                pieces[i] = jnp.where(lower, first, pltpu.roll(second, step * SLOT, 1))
+                pieces[i + step] = jnp.where(
+                    lower, pltpu.roll(first, LANES - step * SLOT, 1), second
+                )
+    return pieces
+
+
+def largest_of_slot(values):
+    lane = lax.broadcasted_iota(jnp.int32, values.shape, 1)
+    for step in (1, 2, 4, 8):
+        partner = jnp.where(
+            jnp.bitwise_and(lane, step) == 0,
+            pltpu.roll(values, LANES - step, 1),
+            pltpu.roll(values, step, 1),
+        )
+        values = jnp.maximum(values, partner)
+    return values
 
 
 def level_of(largest):
@@ -93,8 +122,7 @@
     frame_order = ((peers % GROUP) * GROUP + peers // GROUP)[:, None] == peers[None, :]
     out = np.arange(VOX)
     row, zz, pos = out // (2 * PART), out // 2 % PART, out % 2
-    pick = (zz * 2 * PART + pos * PART + row)[:, None] == out[None, :]
-    panel = places[:, None] == places[None, :] // PART * PART
+    pick = ((zz * 2 + pos) * SLOT + row)[:, None] == np.arange(WIDE)[None, :]
     return dict(
         dft=dft,
         spread=spread.astype(jnp.bfloat16),
@@ -102,7 +130,6 @@
         depth_order=depth_order.astype(jnp.bfloat16),
         frame_order=frame_order.astype(jnp.bfloat16),
         pick=pick.astype(jnp.bfloat16),
-        panel=panel.astype(jnp.bfloat16),
     )
 
 
@@ -291,9 +318,9 @@
 
 
 def model_kernel(
-    images_ref, back_ref, early_ref, ahead_ref, adjoint_ref, coils_hbm, depth_hbm, panel_hbm,
-    out_ref, coils_ref, depth_ref, panel_ref, field_ref, grad_ref,
-    lines_ref, rows_ref, resid_ref, coil_sems, sems,
+    images_ref, back_ref, early_ref, ahead_ref, adjoint_ref, coils_hbm, depth_hbm,
+    out_ref, coils_ref, depth_ref, padded_ref, field_ref, grad_ref,
+    lines_ref, rows_ref, resid_ref, coil_sems, sem,
 ):
     def coil_copy(coil, part):
         return pltpu.make_async_copy(
@@ -307,14 +334,8 @@
     for group in range(2):
         for copy in coil_group(group):
             copy.start()
-    orders = [
-        pltpu.make_async_copy(source, target, sems.at[i])
-        for i, (source, target) in enumerate(
-            [(depth_hbm, depth_ref), (panel_hbm, panel_ref)]
-        )
-    ]
-    for copy in orders:
-        copy.start()
+    order = pltpu.make_async_copy(depth_hbm, depth_ref, sem)
+    order.start()
     for d in range(GROUP):
         here = slice(d * PART, (d + 1) * PART)
         words = images_ref[d]
@@ -384,62 +405,71 @@
             else:
                 grad_ref[0] += grad_re
                 grad_ref[1] += grad_im
-    for copy in orders:
-        copy.wait()
+    order.wait()
+    for d in range(GROUP):
+        at = d * SLOT
+        padded_ref[:, at : at + PART] = grad_ref[:, d * PART : (d + 1) * PART]
+        padded_ref[:, at + PART : at + SLOT] = jnp.zeros((2, SLOT - PART, 2 * N), F32)
     parts = []
     for part in range(2):
         for pos in range(2):
-            high, low = split(grad_ref[part, :, pos * N : (pos + 1) * N])
+            high, low = split(padded_ref[part, :, pos * N : (pos + 1) * N])
             moved = dot(depth_ref[...], high, (1, 1)) + dot(depth_ref[...], low, (1, 1))
-            parts.append(moved.reshape(PART, GROUP, N))
-    largest = functools.reduce(jnp.maximum, map(jnp.abs, parts))
-    largest = jnp.max(largest, axis=0)
-    for shift in (1, 2, 4, 4):
-        ahead = jnp.concatenate([largest[:, shift:], largest[:, :shift]], 1)
-        largest = jnp.maximum(largest, ahead)
-    high, low = split(level_of(largest))
-    level = dot(high, panel_ref[...]) + dot(low, panel_ref[...])
-    scale = scale_down(level)[None]
-    words = [pair_up(parts[pos] * scale, parts[2 + pos] * scale) for pos in range(2)]
-    level = level.astype(jnp.int32)
-    for d in range(GROUP):
-        lanes = slice(d * PART, (d + 1) * PART)
-        pieces = [words[pos][zz, :, lanes] for zz in range(PART) for pos in range(2)]
-        pieces.append(jnp.broadcast_to(level[:, d * PART : d * PART + 1], (GROUP, WIDE - VOX)))
-        out_ref[d * GROUP : (d + 1) * GROUP, 0, :] = jnp.concatenate(pieces, 1)
-
-
-def model(images, back, early, ahead, adjoint, coils, depth_order, panel):
+            parts.append(moved.reshape(PART, GROUP, GROUP * SLOT))
+    largest = jnp.max(functools.reduce(jnp.maximum, map(jnp.abs, parts)), axis=0)
+    lane = lax.broadcasted_iota(jnp.int32, (GROUP, LANES), 1)
+    for half in range(2):
+        lanes = slice(half * LANES, (half + 1) * LANES)
+        level = level_of(largest_of_slot(largest[:, lanes]))
+        scale = scale_down(level)
+        level = level.astype(jnp.int32)
+        words = [
+            jnp.where(
+                jnp.bitwise_and(lane, SLOT - 1) < PART,
+                pair_up(parts[pos][zz, :, lanes] * scale, parts[2 + pos][zz, :, lanes] * scale),
+                level,
+            )
+            for zz in range(PART)
+            for pos in range(2)
+        ]
+        for block in range(WIDE // LANES):
+            swapped = swap_slots(words[block * 8 : (block + 1) * 8])
+            for i, values in enumerate(swapped):
+                at = (half * 8 + i) * GROUP
+                out_ref[at : at + GROUP, 0, block * LANES : (block + 1) * LANES] = values
+
+
+def model(images, back, early, ahead, adjoint, coils, depth_order):
     return pl.pallas_call(
         model_kernel,
         out_shape=jax.ShapeDtypeStruct((GROUP * GROUP, 1, WIDE), jnp.int32),
-        in_specs=[VMEM] * 5 + [HBM] * 3,
+        in_specs=[VMEM] * 5 + [HBM] * 2,
         out_specs=VMEM,
         scratch_shapes=[
             pltpu.VMEM((2, COILS, 2, N, N), BF16),
             pltpu.VMEM((N, N), BF16),
-            pltpu.VMEM((N, N), BF16),
+            pltpu.VMEM((2, GROUP * SLOT, 2 * N), F32),
             pltpu.VMEM((2, N, 2 * N), F32),
             pltpu.VMEM((2, N, 2 * N), F32),
             pltpu.VMEM((4 * LINES, 4 * N), BF16),
             pltpu.VMEM((2 * N, 6 * LINES), BF16),
             pltpu.VMEM((COILS, 6 * LINES, 2 * N), BF16),
             DMA((2, COILS)),
-            DMA((2,)),
+            DMA(()),
         ],
         compiler_params=pltpu.CompilerParams(vmem_limit_bytes=32 * MIB),
         name="model",
     )(
         images,
         *map(in_vmem, (back, early, ahead, adjoint)),
-        *map(in_hbm, (coils, depth_order, panel)),
+        *map(in_hbm, (coils, depth_order)),
     )
 
 
 def update_kernel(grads_ref, weights_ref, pick_ref, slab_ref, out_ref):
     words = grads_ref[:, 0, :].T
-    scale = scale_up(words[VOX : VOX + 1].astype(F32))
-    real, imag = pair_apart(words[0:VOX])
+    scale = scale_up(words[PART : PART + 1].astype(F32))
+    real, imag = pair_apart(words)
     high, low = split(jnp.concatenate([real * scale, imag * scale], 1))
     grad = dot(high, weights_ref[...]) + dot(low, weights_ref[...])
     high, low = split(grad)
@@ -469,7 +499,7 @@
         kspace_data, coil_maps, sampled_lines, table["dft"], flat_temporal, table["frame_order"]
     )
     sent = model(
-        images, back, early, ahead, adjoint, coil_maps, table["depth_order"], table["panel"]
+        images, back, early, ahead, adjoint, coil_maps, table["depth_order"]
     )
     grads = lax.all_to_all(sent, ("dev", "grp"), 0, 0, tiled=True)
     slab = lax.dynamic_slice_in_dim(spatial_basis, lax.axis_index("grp") * PART, PART, 4)

time: 62.4 us -> 61.7 us (0.989)
    pallas_call x1, Pallas kernels: 11.8 us -> 11.1 us  [model(): pl.pallas_call(model_kernel, out_shape=jax.ShapeDtypeStruct((GROUP * GROU...]
  transfers between devices with their start and end apart: 2 -> 2, of which waited for: 2 -> 2; matrix products, arithmetic and copies ran while one was open for 3% -> 4% of each run, Pallas kernels for 9% -> 9%
where the time goes in v5:
time: 61.7 us; the launch traced here: 61.3 us
  Pallas kernels  21 us (34%)
  starting transfers between devices  19.6 us (32%)
  waiting for transfers between devices  18.6 us (30%)
  other arithmetic  1.65 us (3%)
    all_to_all x1, waiting for transfers between devices, on_device(): grads = lax.all_to_all(sent, ('dev', 'grp'), 0, 0, tiled=True)  16.2 us
    all_to_all x1, starting transfers between devices, on_device(): grads = lax.all_to_all(sent, ('dev', 'grp'), 0, 0, tiled=True)  12.7 us
    pallas_call x1, Pallas kernels, model(): pl.pallas_call(model_kernel, out_shape=jax.ShapeDtypeStruct((GROUP * GROU...  11.1 us
    all_to_all x1, starting transfers between devices, on_device(): images = lax.all_to_all(sent, 'dev', 0, 0, tiled=True)  6.84 us
    pallas_call x1, Pallas kernels, data_back(): pl.pallas_call(data_kernel, out_shape=(pltpu.VMEM((COILS, 2 * LINES, 2 *...  5.28 us
    pallas_call x1, Pallas kernels, frames(): pl.pallas_call(frames_kernel, out_shape=jax.ShapeDtypeStruct((GROUP, 40,...  2.81 us
    all_to_all x1, waiting for transfers between devices, on_device(): images = lax.all_to_all(sent, 'dev', 0, 0, tiled=True)  2.33 us
    pallas_call x1, Pallas kernels, update(): pl.pallas_call(update_kernel, out_shape=jax.ShapeDtypeStruct((2, 2 * PART...  1.76 us
  transfers between devices with their start and end apart: 2, of which 2 were waited for; matrix products, arithmetic and copies ran while one was open for 4% of the time, Pallas kernels for 9%

profile of v5, /device:TPU:1, one launch (start us, length us, event | category | flops | bytes accessed | tf_op | source)
XLA Modules:
  0.0 61.3 jit_solution(12830934242755225230)
XLA Ops:
  0.0 2.8 %frames.1 = s32[16,40,128]{2,1,0:T(8,128)} custom-call(bf16[64,12,2,192]{3,2,1,0:T(2,128)(2,1)} %bitcast.11, bf16[64,256]{1,0:T(8,128)(2,1)} %bitcast.12, bf16[64,512]{1,0:T(8,128)(2,1)} %constant.24.clone.spread_hbm, f32[8,512]{1,0:T(8,128)} %constant.25.clone.inside_hbm), custom_call_target="tpu_custom_call" | custom-call | tf_op jit(solution)/shard_map/frames/pallas_call | solution.py:194
  2.8 6.8 %all-to-all-start = ((s32[16,40,128]{2,1,0:T(8,128)}), s32[16,40,128]{2,1,0:T(8,128)S(1)}, u32[]{:S(2)}, u32[]{:S(2)}) async-start(s32[16,40,128]{2,1,0:T(8,128)} %frames.1), calls=%async_computation | async-start | bytes 655360 | tf_op jit(solution)/shard_map/all_to_all | solution.py:497
  9.7 5.3 %data_back.1 = (f32[16,96,384]{2,1,0:T(8,128)S(1)}, bf16[2,1,2,192,192]{4,3,2,1,0:T(8,128)(2,1)S(1)}, bf16[192,384]{1,0:T(8,128)(2,1)S(1)}, bf16[384,192]{1,0:T(8,128)(2,1)S(1)}, bf16[512,64]{1,0:T(8,128)(2,1)S(1)}) custom-call(f32[1,2,16,2,48,192]{5,4,3,2,1,0:T(8,128)} %data_hbm.1, bf16[2,16,2,192,192]{4,3,2,1,0:T(8,128)(2,1)} %coils_hbm.3, ...), custom_call_target="tpu_custom_call" | custom-call | tf_op jit(solution)/shard_map/data_back/pallas_call | solution.py:295
  14.9 2.3 %all-to-all-done.images_ref = s32[16,40,128]{2,1,0:T(8,128)S(1)} async-done(((s32[16,40,128]{2,1,0:T(8,128)}), s32[16,40,128]{2,1,0:T(8,128)S(1)}, u32[]{:S(2)}, u32[]{:S(2)}) %all-to-all-start) | async-done | bytes 327712 | tf_op jit(solution)/shard_map/all_to_all | solution.py:497
  17.3 11.1 %model.1 = s32[256,1,384]{2,1,0:T(1,128)} custom-call(s32[16,40,128]{2,1,0:T(8,128)S(1)} %all-to-all-done.images_ref, f32[16,96,384]{2,1,0:T(8,128)S(1)} %get-tuple-element.10.back_ref, bf16[2,1,2,192,192]{4,3,2,1,0:T(8,128)(2,1)S(1)} %get-tuple-element.11.early_ref, bf16[192,384]{1,0:T(8,128)(2,1)S(1)} %get-tuple-element.12.ahead_ref, ...), custom_call_target="tpu_custom_call" | custom-call | tf_op jit(solution)/shard_map/model/pallas_call | solution.py:443
  28.4 0.0 copy-start
  28.4 12.7 %all-to-all-start.1 = ((s32[256,1,384]{2,1,0:T(1,128)}), s32[256,1,384]{2,1,0:T(1,128)S(1)}, u32[]{:S(2)}, u32[]{:S(2)}) async-start(s32[256,1,384]{2,1,0:T(1,128)} %model.1), calls=%async_computation.1 | async-start | bytes 786432 | tf_op jit(solution)/shard_map/all_to_all | solution.py:504
  41.2 1.6 %convert_bitcast_fusion = f32[2,12,12,2,32]{2,3,1,4,0:T(2,128)S(1)} fusion(bf16[2,32,2,12,192]{4,2,3,1,0:T(2,128)(2,1)} %param.11, s32[]{:T(128)S(6)} %select_n.3), kind=kLoop, calls=%fused_computation | loop fusion | flops 18432 | bytes 110596 | tf_op jit(solution)/shard_map/convert_element_type | solution.py:506
  42.8 0.5 copy.12
  43.4 16.2 %all-to-all-done.1.grads_ref = s32[256,1,384]{2,1,0:T(1,128)S(1)} async-done(((s32[256,1,384]{2,1,0:T(1,128)}), s32[256,1,384]{2,1,0:T(1,128)S(1)}, u32[]{:S(2)}, u32[]{:S(2)}) %all-to-all-start.1) | async-done | bytes 393248 | tf_op jit(solution)/shard_map/all_to_all | solution.py:504
  59.6 0.0 copy-done
  59.6 1.8 %update.1 = f32[2,288,32]{2,1,0:T(8,128)} custom-call(s32[256,1,384]{2,1,0:T(1,128)S(1)} %all-to-all-done.1.grads_ref, bf16[512,64]{1,0:T(8,128)(2,1)S(1)} %get-tuple-element.14.weights_ref, bf16[288,384]{1,0:T(8,128)(2,1)S(1)} %copy-done, f32[2,288,32]{2,1,0:T(8,128)S(1)} %bitcast.10), custom_call_target="tpu_custom_call" | custom-call | tf_op jit(solution)/shard_map/update/pallas_call | solution.py:482
Async XLA Ops:
  2.8 14.5 %all-to-all-start = ((s32[16,40,128]{2,1,0:T(8,128)}), s32[16,40,128]{2,1,0:T(8,128)S(1)}, u32[]{:S(2)}, u32[]{:S(2)}) async-start(s32[16,40,128]{2,1,0:T(8,128)} %frames.1), calls=%async_computation | async-start | bytes 655360 | tf_op jit(solution)/shard_map/all_to_all | solution.py:497
  28.4 31.2 %copy-start = (bf16[288,384]{1,0:T(8,128)(2,1)S(1)}, bf16[288,384]{1,0:T(8,128)(2,1)}, u32[]{:S(2)}) copy-start(bf16[288,384]{1,0:T(8,128)(2,1)} %constant.28.clone.pick_ref) | copy-start | bytes 663556
  28.4 31.2 %all-to-all-start.1 = ((s32[256,1,384]{2,1,0:T(1,128)}), s32[256,1,384]{2,1,0:T(1,128)S(1)}, u32[]{:S(2)}, u32[]{:S(2)}) async-start(s32[256,1,384]{2,1,0:T(1,128)} %model.1), calls=%async_computation.1 | async-start | bytes 786432 | tf_op jit(solution)/shard_map/all_to_all | solution.py:504

commit v6 on v5

--- a/solution.py
+++ b/solution.py
@@ -18,7 +18,7 @@
 LINES = 48
 EARLY = 1
 GROUPS = [[(0,)], [(1, 2)], [(3, 4), (5, 6)], [(7, 8), (9, 10)], [(11, 12), (13, 14), (15,)]]
-CHUNK = 4
+CHUNK = 16
 GROUP = 16
 VOX = 2 * PART * PART
 SLOT = 16
@@ -111,7 +111,8 @@
     angles = (places[:, None] * places[None, :] % N) * (2.0 * math.pi / N)
     cos_pair = two_terms(np.cos(angles) / math.sqrt(N))
     sin_pair = two_terms(np.sin(angles) / math.sqrt(N))
-    dft = np.stack([*cos_pair, *sin_pair])
+    sum_pair = two_terms((np.cos(angles) + np.sin(angles)) / math.sqrt(N))
+    dft = np.stack([*cos_pair, *sin_pair, *sum_pair])
     columns = np.arange(2 * RANK * 2 * ROWS)
     spread = columns[None, :] // (2 * ROWS) == np.arange(2 * RANK)[:, None]
     rows = np.arange(2 * ROWS)
@@ -261,7 +262,8 @@
         adjoint_ref[N : 2 * N, at : at + 48] = sin_back.astype(BF16)
         adjoint_ref[N : 2 * N, at + 48 : at + 96] = cos_back.astype(BF16)
 
-    def through(high, low, which):
+    def through(values, which):
+        high, low = split(values)
         return (
             dot(high, dft_ref[which])
             + dot(low, dft_ref[which])
@@ -271,10 +273,11 @@
     for i in range(COILS // CHUNK):
         chunks[i].wait()
         here = slice(i * CHUNK, (i + 1) * CHUNK)
-        re_high, re_low = split(data_ref[0, here].reshape(CHUNK * 2 * LINES, N))
-        im_high, im_low = split(data_ref[1, here].reshape(CHUNK * 2 * LINES, N))
-        back_re = through(re_high, re_low, 0) - through(im_high, im_low, 2)
-        back_im = through(re_high, re_low, 2) + through(im_high, im_low, 0)
+        data_re = data_ref[0, here].reshape(CHUNK * 2 * LINES, N)
+        data_im = data_ref[1, here].reshape(CHUNK * 2 * LINES, N)
+        by_cos, by_sin = through(data_re, 0), through(data_im, 2)
+        back_re = by_cos - by_sin
+        back_im = through(data_re + data_im, 4) - by_cos - by_sin
         for part, values in enumerate((back_re, back_im)):
             values = values.reshape(CHUNK, 2, LINES, N)
             at = slice(part * LINES, (part + 1) * LINES)
@@ -306,7 +309,7 @@
         scratch_shapes=[
             pltpu.VMEM((2, COILS, 2, LINES, N), F32),
             pltpu.VMEM((1, LINES), jnp.int32),
-            pltpu.VMEM((4, N, N), BF16),
+            pltpu.VMEM((6, N, N), BF16),
             pltpu.VMEM((2 * RANK, GROUP * GROUP), BF16),
             pltpu.VMEM((GROUP * GROUP, GROUP * GROUP), BF16),
             DMA((COILS // CHUNK,)),

time: 61.7 us -> 61.7 us (level)
  Pallas kernels: 21 us -> 20.3 us
    all_to_all x1, waiting for transfers between devices: 2.33 us -> 3 us  [on_device(): images = lax.all_to_all(sent, 'dev', 0, 0, tiled=True)]
    pallas_call x1, Pallas kernels: 5.28 us -> 4.61 us  [data_back(): pl.pallas_call(data_kernel, out_shape=(pltpu.VMEM((COILS, 2 * LINES, 2 *...]
  transfers between devices with their start and end apart: 2 -> 2, of which waited for: 2 -> 2; matrix products, arithmetic and copies ran while one was open for 4% -> 4% of each run, Pallas kernels for 9% -> 8%
where the time goes in v6:
time: 61.7 us; the launch traced here: 61.3 us
  Pallas kernels  20.3 us (33%)
  starting transfers between devices  19.6 us (32%)
  waiting for transfers between devices  19.2 us (31%)
  other arithmetic  1.65 us (3%)
    all_to_all x1, waiting for transfers between devices, on_device(): grads = lax.all_to_all(sent, ('dev', 'grp'), 0, 0, tiled=True)  16.2 us
    all_to_all x1, starting transfers between devices, on_device(): grads = lax.all_to_all(sent, ('dev', 'grp'), 0, 0, tiled=True)  12.7 us
    pallas_call x1, Pallas kernels, model(): pl.pallas_call(model_kernel, out_shape=jax.ShapeDtypeStruct((GROUP * GROU...  11.1 us
    all_to_all x1, starting transfers between devices, on_device(): images = lax.all_to_all(sent, 'dev', 0, 0, tiled=True)  6.84 us
    pallas_call x1, Pallas kernels, data_back(): pl.pallas_call(data_kernel, out_shape=(pltpu.VMEM((COILS, 2 * LINES, 2 *...  4.61 us
    all_to_all x1, waiting for transfers between devices, on_device(): images = lax.all_to_all(sent, 'dev', 0, 0, tiled=True)  3 us
    pallas_call x1, Pallas kernels, frames(): pl.pallas_call(frames_kernel, out_shape=jax.ShapeDtypeStruct((GROUP, 40,...  2.81 us
    pallas_call x1, Pallas kernels, update(): pl.pallas_call(update_kernel, out_shape=jax.ShapeDtypeStruct((2, 2 * PART...  1.76 us
  transfers between devices with their start and end apart: 2, of which 2 were waited for; matrix products, arithmetic and copies ran while one was open for 4% of the time, Pallas kernels for 8%

profile of v6, /device:TPU:1, one launch (start us, length us, event | category | flops | bytes accessed | tf_op | source)
XLA Modules:
  0.0 61.3 jit_solution(11119878563682247672)
XLA Ops:
  0.0 2.8 %frames.1 = s32[16,40,128]{2,1,0:T(8,128)} custom-call(bf16[64,12,2,192]{3,2,1,0:T(2,128)(2,1)} %bitcast.11, bf16[64,256]{1,0:T(8,128)(2,1)} %bitcast.12, bf16[64,512]{1,0:T(8,128)(2,1)} %constant.24.clone.spread_hbm, f32[8,512]{1,0:T(8,128)} %constant.25.clone.inside_hbm), custom_call_target="tpu_custom_call" | custom-call | tf_op jit(solution)/shard_map/frames/pallas_call | solution.py:195
  2.8 6.8 %all-to-all-start = ((s32[16,40,128]{2,1,0:T(8,128)}), s32[16,40,128]{2,1,0:T(8,128)S(1)}, u32[]{:S(2)}, u32[]{:S(2)}) async-start(s32[16,40,128]{2,1,0:T(8,128)} %frames.1), calls=%async_computation | async-start | bytes 655360 | tf_op jit(solution)/shard_map/all_to_all | solution.py:500
  9.7 4.6 %data_back.1 = (f32[16,96,384]{2,1,0:T(8,128)S(1)}, bf16[2,1,2,192,192]{4,3,2,1,0:T(8,128)(2,1)S(1)}, bf16[192,384]{1,0:T(8,128)(2,1)S(1)}, bf16[384,192]{1,0:T(8,128)(2,1)S(1)}, bf16[512,64]{1,0:T(8,128)(2,1)S(1)}) custom-call(f32[1,2,16,2,48,192]{5,4,3,2,1,0:T(8,128)} %data_hbm.1, bf16[2,16,2,192,192]{4,3,2,1,0:T(8,128)(2,1)} %coils_hbm.3, ...), custom_call_target="tpu_custom_call" | custom-call | tf_op jit(solution)/shard_map/data_back/pallas_call | solution.py:298
  14.3 3.0 %all-to-all-done.images_ref = s32[16,40,128]{2,1,0:T(8,128)S(1)} async-done(((s32[16,40,128]{2,1,0:T(8,128)}), s32[16,40,128]{2,1,0:T(8,128)S(1)}, u32[]{:S(2)}, u32[]{:S(2)}) %all-to-all-start) | async-done | bytes 327712 | tf_op jit(solution)/shard_map/all_to_all | solution.py:500
  17.3 11.1 %model.1 = s32[256,1,384]{2,1,0:T(1,128)} custom-call(s32[16,40,128]{2,1,0:T(8,128)S(1)} %all-to-all-done.images_ref, f32[16,96,384]{2,1,0:T(8,128)S(1)} %get-tuple-element.10.back_ref, bf16[2,1,2,192,192]{4,3,2,1,0:T(8,128)(2,1)S(1)} %get-tuple-element.11.early_ref, bf16[192,384]{1,0:T(8,128)(2,1)S(1)} %get-tuple-element.12.ahead_ref, ...), custom_call_target="tpu_custom_call" | custom-call | tf_op jit(solution)/shard_map/model/pallas_call | solution.py:446
  28.4 0.0 copy-start
  28.4 12.7 %all-to-all-start.1 = ((s32[256,1,384]{2,1,0:T(1,128)}), s32[256,1,384]{2,1,0:T(1,128)S(1)}, u32[]{:S(2)}, u32[]{:S(2)}) async-start(s32[256,1,384]{2,1,0:T(1,128)} %model.1), calls=%async_computation.1 | async-start | bytes 786432 | tf_op jit(solution)/shard_map/all_to_all | solution.py:507
  41.2 1.6 %convert_bitcast_fusion = f32[2,12,12,2,32]{2,3,1,4,0:T(2,128)S(1)} fusion(bf16[2,32,2,12,192]{4,2,3,1,0:T(2,128)(2,1)} %param.11, s32[]{:T(128)S(6)} %select_n.3), kind=kLoop, calls=%fused_computation | loop fusion | flops 18432 | bytes 110596 | tf_op jit(solution)/shard_map/convert_element_type | solution.py:509
  42.8 0.5 copy.12
  43.4 16.2 %all-to-all-done.1.grads_ref = s32[256,1,384]{2,1,0:T(1,128)S(1)} async-done(((s32[256,1,384]{2,1,0:T(1,128)}), s32[256,1,384]{2,1,0:T(1,128)S(1)}, u32[]{:S(2)}, u32[]{:S(2)}) %all-to-all-start.1) | async-done | bytes 393248 | tf_op jit(solution)/shard_map/all_to_all | solution.py:507
  59.6 0.0 copy-done
  59.6 1.8 %update.1 = f32[2,288,32]{2,1,0:T(8,128)} custom-call(s32[256,1,384]{2,1,0:T(1,128)S(1)} %all-to-all-done.1.grads_ref, bf16[512,64]{1,0:T(8,128)(2,1)S(1)} %get-tuple-element.14.weights_ref, bf16[288,384]{1,0:T(8,128)(2,1)S(1)} %copy-done, f32[2,288,32]{2,1,0:T(8,128)S(1)} %bitcast.10), custom_call_target="tpu_custom_call" | custom-call | tf_op jit(solution)/shard_map/update/pallas_call | solution.py:485
Async XLA Ops:
  2.8 14.5 %all-to-all-start = ((s32[16,40,128]{2,1,0:T(8,128)}), s32[16,40,128]{2,1,0:T(8,128)S(1)}, u32[]{:S(2)}, u32[]{:S(2)}) async-start(s32[16,40,128]{2,1,0:T(8,128)} %frames.1), calls=%async_computation | async-start | bytes 655360 | tf_op jit(solution)/shard_map/all_to_all | solution.py:500
  28.4 31.2 %copy-start = (bf16[288,384]{1,0:T(8,128)(2,1)S(1)}, bf16[288,384]{1,0:T(8,128)(2,1)}, u32[]{:S(2)}) copy-start(bf16[288,384]{1,0:T(8,128)(2,1)} %constant.28.clone.pick_ref) | copy-start | bytes 663556
  28.4 31.2 %all-to-all-start.1 = ((s32[256,1,384]{2,1,0:T(1,128)}), s32[256,1,384]{2,1,0:T(1,128)S(1)}, u32[]{:S(2)}, u32[]{:S(2)}) async-start(s32[256,1,384]{2,1,0:T(1,128)} %model.1), calls=%async_computation.1 | async-start | bytes 786432 | tf_op jit(solution)/shard_map/all_to_all | solution.py:507

commit v7 on v6

--- a/solution.py
+++ b/solution.py
@@ -400,14 +400,13 @@
                 copy.start()
         for coils in pairs:
             go_ahead(coils)
-    for group, pairs in enumerate(GROUPS):
-        for i, coils in enumerate(pairs):
-            grad_re, grad_im = go_back(coils)
-            if group == i == 0:
-                grad_ref[0], grad_ref[1] = grad_re, grad_im
-            else:
-                grad_ref[0] += grad_re
-                grad_ref[1] += grad_im
+    for first in range(0, COILS, 4):
+        grad_re, grad_im = go_back(range(first, first + 4))
+        if first == 0:
+            grad_ref[0], grad_ref[1] = grad_re, grad_im
+        else:
+            grad_ref[0] += grad_re
+            grad_ref[1] += grad_im
     order.wait()
     for d in range(GROUP):
         at = d * SLOT

time: 61.7 us -> 61.5 us (level)
  no operation moved by 1% of the time
where the time goes in v7:
time: 61.5 us; the launch traced here: 61.2 us
  Pallas kernels  20.2 us (33%)
  starting transfers between devices  19.6 us (32%)
  waiting for transfers between devices  19.2 us (31%)
  other arithmetic  1.65 us (3%)
    all_to_all x1, waiting for transfers between devices, on_device(): grads = lax.all_to_all(sent, ('dev', 'grp'), 0, 0, tiled=True)  16.2 us
    all_to_all x1, starting transfers between devices, on_device(): grads = lax.all_to_all(sent, ('dev', 'grp'), 0, 0, tiled=True)  12.7 us
    pallas_call x1, Pallas kernels, model(): pl.pallas_call(model_kernel, out_shape=jax.ShapeDtypeStruct((GROUP * GROU...  11 us
    all_to_all x1, starting transfers between devices, on_device(): images = lax.all_to_all(sent, 'dev', 0, 0, tiled=True)  6.84 us
    pallas_call x1, Pallas kernels, data_back(): pl.pallas_call(data_kernel, out_shape=(pltpu.VMEM((COILS, 2 * LINES, 2 *...  4.61 us
    all_to_all x1, waiting for transfers between devices, on_device(): images = lax.all_to_all(sent, 'dev', 0, 0, tiled=True)  3 us
    pallas_call x1, Pallas kernels, frames(): pl.pallas_call(frames_kernel, out_shape=jax.ShapeDtypeStruct((GROUP, 40,...  2.81 us
    pallas_call x1, Pallas kernels, update(): pl.pallas_call(update_kernel, out_shape=jax.ShapeDtypeStruct((2, 2 * PART...  1.76 us
  transfers between devices with their start and end apart: 2, of which 2 were waited for; matrix products, arithmetic and copies ran while one was open for 4% of the time, Pallas kernels for 8%

profile of v7, /device:TPU:1, one launch (start us, length us, event | category | flops | bytes accessed | tf_op | source)
XLA Modules:
  0.0 61.2 jit_solution(3653263508555116797)
XLA Ops:
  0.0 2.8 %frames.1 = s32[16,40,128]{2,1,0:T(8,128)} custom-call(bf16[64,12,2,192]{3,2,1,0:T(2,128)(2,1)} %bitcast.11, bf16[64,256]{1,0:T(8,128)(2,1)} %bitcast.12, bf16[64,512]{1,0:T(8,128)(2,1)} %constant.24.clone.spread_hbm, f32[8,512]{1,0:T(8,128)} %constant.25.clone.inside_hbm), custom_call_target="tpu_custom_call" | custom-call | tf_op jit(solution)/shard_map/frames/pallas_call | solution.py:195
  2.8 6.8 %all-to-all-start = ((s32[16,40,128]{2,1,0:T(8,128)}), s32[16,40,128]{2,1,0:T(8,128)S(1)}, u32[]{:S(2)}, u32[]{:S(2)}) async-start(s32[16,40,128]{2,1,0:T(8,128)} %frames.1), calls=%async_computation | async-start | bytes 655360 | tf_op jit(solution)/shard_map/all_to_all | solution.py:499
  9.7 4.6 %data_back.1 = (f32[16,96,384]{2,1,0:T(8,128)S(1)}, bf16[2,1,2,192,192]{4,3,2,1,0:T(8,128)(2,1)S(1)}, bf16[192,384]{1,0:T(8,128)(2,1)S(1)}, bf16[384,192]{1,0:T(8,128)(2,1)S(1)}, bf16[512,64]{1,0:T(8,128)(2,1)S(1)}) custom-call(f32[1,2,16,2,48,192]{5,4,3,2,1,0:T(8,128)} %data_hbm.1, bf16[2,16,2,192,192]{4,3,2,1,0:T(8,128)(2,1)} %coils_hbm.3, ...), custom_call_target="tpu_custom_call" | custom-call | tf_op jit(solution)/shard_map/data_back/pallas_call | solution.py:298
  14.3 3.0 %all-to-all-done.images_ref = s32[16,40,128]{2,1,0:T(8,128)S(1)} async-done(((s32[16,40,128]{2,1,0:T(8,128)}), s32[16,40,128]{2,1,0:T(8,128)S(1)}, u32[]{:S(2)}, u32[]{:S(2)}) %all-to-all-start) | async-done | bytes 327712 | tf_op jit(solution)/shard_map/all_to_all | solution.py:499
  17.3 11.0 %model.1 = s32[256,1,384]{2,1,0:T(1,128)} custom-call(s32[16,40,128]{2,1,0:T(8,128)S(1)} %all-to-all-done.images_ref, f32[16,96,384]{2,1,0:T(8,128)S(1)} %get-tuple-element.10.back_ref, bf16[2,1,2,192,192]{4,3,2,1,0:T(8,128)(2,1)S(1)} %get-tuple-element.11.early_ref, bf16[192,384]{1,0:T(8,128)(2,1)S(1)} %get-tuple-element.12.ahead_ref, ...), custom_call_target="tpu_custom_call" | custom-call | tf_op jit(solution)/shard_map/model/pallas_call | solution.py:445
  28.3 0.0 copy-start
  28.3 12.7 %all-to-all-start.1 = ((s32[256,1,384]{2,1,0:T(1,128)}), s32[256,1,384]{2,1,0:T(1,128)S(1)}, u32[]{:S(2)}, u32[]{:S(2)}) async-start(s32[256,1,384]{2,1,0:T(1,128)} %model.1), calls=%async_computation.1 | async-start | bytes 786432 | tf_op jit(solution)/shard_map/all_to_all | solution.py:506
  41.1 1.6 %convert_bitcast_fusion = f32[2,12,12,2,32]{2,3,1,4,0:T(2,128)S(1)} fusion(bf16[2,32,2,12,192]{4,2,3,1,0:T(2,128)(2,1)} %param.11, s32[]{:T(128)S(6)} %select_n.3), kind=kLoop, calls=%fused_computation | loop fusion | flops 18432 | bytes 110596 | tf_op jit(solution)/shard_map/convert_element_type | solution.py:508
  42.7 0.5 copy.12
  43.2 16.2 %all-to-all-done.1.grads_ref = s32[256,1,384]{2,1,0:T(1,128)S(1)} async-done(((s32[256,1,384]{2,1,0:T(1,128)}), s32[256,1,384]{2,1,0:T(1,128)S(1)}, u32[]{:S(2)}, u32[]{:S(2)}) %all-to-all-start.1) | async-done | bytes 393248 | tf_op jit(solution)/shard_map/all_to_all | solution.py:506
  59.5 0.0 copy-done
  59.5 1.8 %update.1 = f32[2,288,32]{2,1,0:T(8,128)} custom-call(s32[256,1,384]{2,1,0:T(1,128)S(1)} %all-to-all-done.1.grads_ref, bf16[512,64]{1,0:T(8,128)(2,1)S(1)} %get-tuple-element.14.weights_ref, bf16[288,384]{1,0:T(8,128)(2,1)S(1)} %copy-done, f32[2,288,32]{2,1,0:T(8,128)S(1)} %bitcast.10), custom_call_target="tpu_custom_call" | custom-call | tf_op jit(solution)/shard_map/update/pallas_call | solution.py:484
Async XLA Ops:
  2.8 14.5 %all-to-all-start = ((s32[16,40,128]{2,1,0:T(8,128)}), s32[16,40,128]{2,1,0:T(8,128)S(1)}, u32[]{:S(2)}, u32[]{:S(2)}) async-start(s32[16,40,128]{2,1,0:T(8,128)} %frames.1), calls=%async_computation | async-start | bytes 655360 | tf_op jit(solution)/shard_map/all_to_all | solution.py:499
  28.3 31.2 %copy-start = (bf16[288,384]{1,0:T(8,128)(2,1)S(1)}, bf16[288,384]{1,0:T(8,128)(2,1)}, u32[]{:S(2)}) copy-start(bf16[288,384]{1,0:T(8,128)(2,1)} %constant.28.clone.pick_ref) | copy-start | bytes 663556
  28.3 31.2 %all-to-all-start.1 = ((s32[256,1,384]{2,1,0:T(1,128)}), s32[256,1,384]{2,1,0:T(1,128)S(1)}, u32[]{:S(2)}, u32[]{:S(2)}) async-start(s32[256,1,384]{2,1,0:T(1,128)} %model.1), calls=%async_computation.1 | async-start | bytes 786432 | tf_op jit(solution)/shard_map/all_to_all | solution.py:506
